TPU v7x, 256 devices: a whole 4x4x8 slice. The times are simulated.
256 devices in a mesh: ctx: 32 (over x, z_lo, core), tp: 8 (over z_hi, y).
Axes of the slice: x: 4, y: 4, z: 8 (z_hi: 2, z_lo: 4; z = z_hi * 4 + z_lo), core: 2. Of those that a mesh axis runs over, the one named last changes fastest.
Arguments:
- tokens: bfloat16 [16384, 4096], P('ctx', 'tp'), may hold values from -6 to 6
- norm_gain: float32 [4096], replicated, may hold values from 0.5 to 1.5
- w_in: bfloat16 [4096, 3, 2048], P(None, None, 'tp'), may hold values from -0.09375 to 0.09375
- w_short: float32 [3, 3, 2048], P(None, None, 'tp'), may hold values from -3 to 3
- residues: float32 [2048, 16], P('tp'), may hold values from -0.15625 to 0.15625
- decays: float32 [2048, 16], P('tp'), may hold values from 6.1035156e-05 to 0.05
- direct: float32 [2048], P('tp'), may hold values from -3 to 3
- w_out: bfloat16 [2048, 4096], P('tp'), may hold values from -0.1875 to 0.1875
Outputs:
- mixed: bfloat16 [16384, 4096], P('ctx', 'tp')
All inputs are finite; a program needn't handle non-finite values.
Results may differ from a plain program's by a relative error of at most 0.02.
Values may be sent and summed in bfloat16 or wider, within the bound.
A program may use at most 128 MiB of HBM per device.

v0:
```python
import math

import jax
import jax.numpy as jnp
from jax import lax
from jax.sharding import PartitionSpec as P

precise = lax.Precision.HIGHEST


def passed_along(block, axis, distance):
    devices = range(lax.axis_size(axis))
    route = [(i - distance, i) for i in devices if i - distance in devices]
    return lax.ppermute(block, axis, route)


def swapped(array, axis, distance):
    return lax.ppermute(array, axis, [(i, i ^ 1 << distance) for i in range(lax.axis_size(axis))])


def cmatmul(form, table_cos, table_sin, real_part, imag_part):

    def contract(table, values):
        return jnp.einsum(form, table, values, precision=precise)

    return (
        contract(table_cos, real_part) - contract(table_sin, imag_part),
        contract(table_sin, real_part) + contract(table_cos, imag_part),
    )


def tables(length, sign):
    index = lax.broadcasted_iota(jnp.int32, (length, length), 0)
    other = lax.broadcasted_iota(jnp.int32, (length, length), 1)
    angle = sign * 2.0 * math.pi * (index * other % length).astype(jnp.float32) / length
    return (jnp.cos(angle), jnp.sin(angle))


def dft_rows(real_part, imag_part, sign):
    table_cos, table_sin = tables(real_part.shape[-2], sign)
    return cmatmul("sr,...sc->...rc", table_cos, table_sin, real_part, imag_part)


def rotate(real_part, imag_part, angle):
    cosine = jnp.cos(angle)
    sine = jnp.sin(angle)
    return (real_part * cosine - imag_part * sine, real_part * sine + imag_part * cosine)


def twiddle(real_part, imag_part, column, length, sign):
    offsets = lax.broadcasted_iota(jnp.int32, (real_part.shape[-2], 1), 0)
    angle = sign * 2.0 * math.pi * (offsets * column % length).astype(jnp.float32) / length
    return rotate(real_part, imag_part, angle)


def spectrum(freq, mode_weights, mode_rates, length):
    theta = math.pi * freq.astype(jnp.float32) / length
    parity = 1.0 - 2.0 * (freq % 2).astype(jnp.float32)
    half_sine = jnp.sin(0.5 * theta)
    sine = jnp.sin(theta)
    acc_real = jnp.zeros((), jnp.float32)
    acc_imag = jnp.zeros((), jnp.float32)
    for order_index in range(mode_weights.shape[0]):
        rate = mode_rates[order_index]
        weight_mode = mode_weights[order_index]
        factor = jnp.exp(-rate)
        spacing = -jnp.expm1(-rate)
        remain = jnp.exp(-rate * length)
        numer = weight_mode * (1.0 - remain * parity)
        den_real = spacing + factor * 2.0 * half_sine * half_sine
        den_imag = factor * sine
        magnitude = den_real * den_real + den_imag * den_imag
        acc_real = acc_real + numer * den_real / magnitude
        acc_imag = acc_imag - numer * den_imag / magnitude
    return (acc_real, acc_imag)


def cproduct(real_part, imag_part, spec_real, spec_imag):
    return (
        real_part * spec_real - imag_part * spec_imag,
        real_part * spec_imag + imag_part * spec_real,
    )


def local(tokens, norm_gain, w_in, w_short, residues, decays, direct, w_out):
    whole_rows = lax.all_gather(tokens, "tp", axis=1, tiled=True)
    values = whole_rows.astype(jnp.float32)
    meansq = jnp.mean(values * values, axis=-1, keepdims=True)
    normed = (values * lax.rsqrt(meansq + 1e-06) * norm_gain[None, :]).astype(jnp.bfloat16)
    width = w_in.shape[2]
    rows = tokens.shape[0]
    proj = jnp.dot(
        normed, w_in.reshape(w_in.shape[0], 3 * width), preferred_element_type=jnp.float32
    )
    proj = proj.astype(jnp.bfloat16).reshape(rows, 3, width)
    reach = w_short.shape[0] - 1
    earlier = passed_along(proj[rows - reach :], "ctx", 1)
    extended = jnp.concatenate([earlier, proj], axis=0).astype(jnp.float32)
    short = jnp.zeros((rows, 3, width), jnp.float32)
    for tap in range(reach + 1):
        short = short + w_short[tap][None, :, :] * extended[reach - tap : reach - tap + rows]
    gate_q = short[:, 0, :]
    mixed_in = short[:, 1, :] * short[:, 2, :]
    device = lax.axis_index("ctx")
    count = lax.axis_size("ctx")
    span = rows * count
    padded_len = 2 * span
    halves = lax.broadcasted_iota(jnp.int32, (2, 1, 1), 0)
    position = device * rows + lax.broadcasted_iota(jnp.int32, (rows, 1), 0)
    phase = 2.0 * math.pi * position.astype(jnp.float32) / padded_len
    real_part = jnp.stack([mixed_in, mixed_in * jnp.cos(phase)])
    imag_part = jnp.stack([jnp.zeros_like(mixed_in), -mixed_in * jnp.sin(phase)])
    nbits = count.bit_length() - 1
    for section_bit in reversed(range(nbits)):
        half = 1 << section_bit
        other_real, other_imag = (
            swapped(real_part.astype(jnp.bfloat16), "ctx", section_bit).astype(real_part.dtype),
            swapped(imag_part.astype(jnp.bfloat16), "ctx", section_bit).astype(imag_part.dtype),
        )
        upper = device // half % 2 == 1
        angle = -math.pi * (device % half).astype(jnp.float32) / half
        cosine = jnp.cos(angle)
        sine = jnp.sin(angle)
        diff_real = other_real - real_part
        diff_imag = other_imag - imag_part
        real_part, imag_part = (
            jnp.where(upper, diff_real * cosine - diff_imag * sine, real_part + other_real),
            jnp.where(upper, diff_real * sine + diff_imag * cosine, imag_part + other_imag),
        )
    column = jnp.zeros((), jnp.int32)
    for section_bit in range(nbits):
        column = column + device // (1 << section_bit) % 2 * (1 << nbits - 1 - section_bit)
    real_part, imag_part = twiddle(real_part, imag_part, column, span, -1.0)
    real_part, imag_part = dft_rows(real_part, imag_part, -1.0)
    row_index = lax.broadcasted_iota(jnp.int32, (rows, 1), 0)
    freq = 2 * (column + count * row_index) + halves
    spec_real, spec_imag = spectrum(freq, residues.T, decays.T, span)
    real_part, imag_part = cproduct(real_part, imag_part, spec_real, spec_imag)
    real_part, imag_part = dft_rows(real_part, imag_part, 1.0)
    real_part, imag_part = twiddle(real_part, imag_part, column, span, 1.0)
    for section_bit in range(nbits):
        half = 1 << section_bit
        other_real, other_imag = (
            swapped(real_part.astype(jnp.bfloat16), "ctx", section_bit).astype(real_part.dtype),
            swapped(imag_part.astype(jnp.bfloat16), "ctx", section_bit).astype(imag_part.dtype),
        )
        upper = device // half % 2 == 1
        angle = math.pi * (device % half).astype(jnp.float32) / half
        cosine = jnp.cos(angle)
        sine = jnp.sin(angle)
        turned_other_real = other_real * cosine - other_imag * sine
        turned_other_imag = other_real * sine + other_imag * cosine
        turned_real = real_part * cosine - imag_part * sine
        turned_imag = real_part * sine + imag_part * cosine
        real_part, imag_part = (
            jnp.where(upper, other_real - turned_real, real_part + turned_other_real),
            jnp.where(upper, other_imag - turned_imag, imag_part + turned_other_imag),
        )
    convolved = (
        real_part[0] + jnp.cos(phase) * real_part[1] - jnp.sin(phase) * imag_part[1]
    ) / padded_len
    gated = (gate_q * (convolved + direct[None, :] * mixed_in)).astype(jnp.bfloat16)
    terms = jnp.dot(gated, w_out, preferred_element_type=jnp.float32)
    return lax.psum_scatter(terms.astype(jnp.bfloat16), "tp", scatter_dimension=1, tiled=True)


def solution(mesh):
    placed = (
        P("ctx", "tp"),
        P(),
        P(None, None, "tp"),
        P(None, None, "tp"),
        P("tp", None),
        P("tp", None),
        P("tp"),
        P("tp", None),
    )
    return jax.shard_map(
        local, mesh=mesh, in_specs=placed, out_specs=P("ctx", "tp"), check_vma=False
    )
```

profile of v0, /device:TPU:2, one launch (start us, length us, event | category | flops | bytes accessed | tf_op | source)
XLA Modules:
  0.0 614.9 jit_solution(381467125737578728)
XLA Ops:
  7.3 8.6 %copy.11 = bf16[4096,3,256]{0,2,1:T(8,128)(2,1)} copy(bf16[4096,3,256]{2,0,1:T(8,128)(2,1)} %param.10) | data formatting | bytes 12582912 | tf_op args[2]
  16.0 108.3 %all-gather.2.cloned.1.call-done = bf16[512,4096]{1,0:T(8,128)(2,1)} async-done(((bf16[512,512]{1,0:T(8,128)(2,1)}), bf16[512,4096]{1,0:T(8,128)(2,1)}) %all-gather.2.cloned.1.call-update) | async-done | bytes 4194320 | tf_op jit(solution)/shard_map/all_gather | solution.py:86
  124.3 3.2 fusion
  127.8 6.2 %fusion.9 = bf16[512,768]{1,0:T(8,128)(2,1)S(1)} fusion(bf16[4096,768]{0,1:T(8,128)(2,1)} %bitcast.172, bf16[512,4096]{1,0:T(8,128)(2,1)S(1)} %copy-done.4, f32[4096]{0:T(1024)S(1)} %copy-done.12, f32[512]{0:T(512)S(1)} %add_rsqrt_fusion), kind=kOutput, calls=%fused_computation.76 | convolution fusion | flops 3230007296 | bytes 11290624 | tf_op jit(solution)/shard_map/dot_general | solution.py:92
  135.2 1.9 collective-permute-start
  138.6 6.3 %collective-permute-done = bf16[2,3,256]{0,2,1:T(8,128)(2,1)S(1)} collective-permute-done((bf16[2,3,256]{0,2,1:T(8,128)(2,1)S(1)}, bf16[2,3,256]{0,2,1:T(8,128)(2,1)S(1)}, u32[]{:S(2)}, u32[]{:S(2)}) %collective-permute-start) | collective-permute-done | bytes 3104 | tf_op jit(solution)/shard_map/ppermute | solution.py:14
  147.8 2.1 collective-permute-start.1
  150.9 1.5 collective-permute-start.2
  152.6 11.9 %collective-permute-done.1 = bf16[2,512,256]{1,2,0:T(8,128)(2,1)} collective-permute-done((bf16[2,512,256]{1,2,0:T(8,128)(2,1)}, bf16[2,512,256]{1,2,0:T(8,128)(2,1)}, u32[]{:S(2)}, u32[]{:S(2)}) %collective-permute-start.1) | collective-permute-done | bytes 524320 | tf_op jit(solution)/shard_map/ppermute | solution.py:18
  164.5 5.8 collective-permute-done.2
  170.3 3.5 fusion.238
  174.3 1.5 collective-permute-start.4
  176.4 11.7 %collective-permute-done.3 = bf16[2,512,256]{1,2,0:T(8,128)(2,1)S(1)} collective-permute-done((bf16[2,512,256]{1,2,0:T(8,128)(2,1)}, bf16[2,512,256]{1,2,0:T(8,128)(2,1)S(1)}, u32[]{:S(2)}, u32[]{:S(2)}) %collective-permute-start.3) | collective-permute-done | bytes 524320 | tf_op jit(solution)/shard_map/ppermute | solution.py:18
  188.1 5.6 collective-permute-done.4
  193.8 2.1 fusion.234
  195.9 13.6 %collective-permute-start.6 = (bf16[2,512,256]{1,2,0:T(8,128)(2,1)S(1)}, bf16[2,512,256]{1,2,0:T(8,128)(2,1)S(1)}, u32[]{:S(2)}, u32[]{:S(2)}) collective-permute-start(bf16[2,512,256]{1,2,0:T(8,128)(2,1)S(1)} %get-tuple-element.60), channel_id=1, source_target_pairs={{0,32},{8,40},{16,48},{24,56},{32,0},{40,8},{48,16},{56,24},{64,96... | collective-permute-start | bytes 1572872 | tf_op jit(solution)/shard_map/ppermute | solution.py:18
  209.6 24.0 %collective-permute-done.5 = bf16[2,512,256]{1,2,0:T(8,128)(2,1)S(1)} collective-permute-done((bf16[2,512,256]{1,2,0:T(8,128)(2,1)S(1)}, bf16[2,512,256]{1,2,0:T(8,128)(2,1)S(1)}, u32[]{:S(2)}, u32[]{:S(2)}) %collective-permute-start.5) | collective-permute-done | bytes 524320 | tf_op jit(solution)/shard_map/ppermute | solution.py:18
  233.6 6.1 collective-permute-done.6
  240.4 2.0 collective-permute-start.8
  242.5 12.7 %collective-permute-done.7 = bf16[2,512,256]{1,2,0:T(8,128)(2,1)S(1)} collective-permute-done((bf16[2,512,256]{1,2,0:T(8,128)(2,1)S(1)}, bf16[2,512,256]{1,2,0:T(8,128)(2,1)S(1)}, u32[]{:S(2)}, u32[]{:S(2)}) %collective-permute-start.7) | collective-permute-done | bytes 524320 | tf_op jit(solution)/shard_map/ppermute | solution.py:18
  255.2 7.0 %collective-permute-done.8 = bf16[2,512,256]{1,2,0:T(8,128)(2,1)S(1)} collective-permute-done((bf16[2,512,256]{1,2,0:T(8,128)(2,1)S(1)}, bf16[2,512,256]{1,2,0:T(8,128)(2,1)S(1)}, u32[]{:S(2)}, u32[]{:S(2)}) %collective-permute-start.8) | collective-permute-done | bytes 524320 | tf_op jit(solution)/shard_map/ppermute | solution.py:18
  265.9 5.8 fusion.103
  271.7 6.2 %fusion.107 = f32[2,256,512]{2,1,0:T(8,128)S(1)} fusion(f32[2,512,256]{1,2,0:T(8,128)S(1)} %get-tuple-element.55, f32[2,512,256]{1,2,0:T(8,128)S(1)} %get-tuple-element.54, f32[512]{0:T(512)S(1)} %get-tuple-element.139, f32[512]{0:T(512)S(1)} %get-tuple-element.140), kind=kOutput, calls=%fused_computation.200 | convolution fusion | flops 1615069184 | bytes 3149824 | tf_op jit(solution)/shard_map/sr,...sc->...rc/dot_general | solution.py:24
  277.9 5.8 fusion.13
  283.8 16.4 %multiply_add_fusion.1 = (f32[2,512,256]{1,2,0:T(8,128)S(1)}, f32[2,512,256]{1,2,0:T(8,128)S(1)}, f32[2,512,256]{1,2,0:T(8,128)S(1)}, f32[2,512,256]{1,2,0:T(8,128)S(1)}) fusion(f32[2,512,256]{1,2,0:T(8,128)S(1)} %fusion.13, f32[256]{0:T(256)S(1)} %bitcast.194, f32[256]{0:T(256)S(1)} %get-tuple-element.141, f32[256]{0:T(256)S(1)} %bitcast.250, ...), kind=kOutput, calls=%fused_computation.205 | convolution fusion | flops 1682964480 | bytes 8486912 | tf_op jit(solution)/shard_map/sr,...sc->...rc/dot_general | solution.py:24
  300.6 6.3 %fusion.101 = f32[2,256,512]{2,1,0:T(8,128)S(1)} fusion(f32[2,512,256]{1,2,0:T(8,128)S(1)} %multiply_subtract_fusion.1), kind=kOutput, calls=%fused_computation.194 | convolution fusion | flops 1614282752 | bytes 2097152 | tf_op jit(solution)/shard_map/sr,...sc->...rc/dot_general | solution.py:24
  307.0 6.3 %fusion.97 = f32[2,256,512]{2,1,0:T(8,128)S(1)} fusion(f32[2,512,256]{1,2,0:T(8,128)S(1)} %multiply_subtract_fusion.1), kind=kOutput, calls=%fused_computation.190 | convolution fusion | flops 1614282752 | bytes 2097152 | tf_op jit(solution)/shard_map/sr,...sc->...rc/dot_general | solution.py:24
  313.3 6.3 %convolution_subtract_fusion = f32[2,256,512]{2,1,0:T(8,128)S(1)} fusion(f32[2,256,512]{2,1,0:T(8,128)S(1)} %fusion.101, f32[2,512,256]{1,2,0:T(8,128)S(1)} %get-tuple-element.25), kind=kOutput, calls=%fused_computation.78 | convolution fusion | flops 1614544896 | bytes 3145728 | tf_op jit(solution)/shard_map/sr,...sc->...rc/dot_general | solution.py:24
  319.6 6.7 %bitcast_convert_fusion.1 = (bf16[2,512,256]{1,2,0:T(8,128)(2,1)S(1)}, f32[2,256,512]{2,1,0:T(8,128)S(1)}, bf16[2,512,256]{1,2,0:T(8,128)(2,1)S(1)}, f32[2,256,512]{2,1,0:T(8,128)S(1)}) fusion(f32[512]{0:T(512)S(1)} %get-tuple-element.137, f32[2,256,512]{2,1,0:T(8,128)S(1)} %convolution_subtract_fusion, f32[512]{0:T(512)S(1)} %get-tuple-element.138, ...), kind=kOutput, calls=%fused_computation.189 | convolution fusion | flops 1616642048 | bytes 6295552 | tf_op jit(solution)/shard_map/sr,...sc->...rc/dot_general | solution.py:24
  329.1 1.7 fusion.221
  330.8 1.5 collective-permute-start.13
  333.0 12.9 %collective-permute-done.13 = bf16[2,512,256]{1,2,0:T(8,128)(2,1)} collective-permute-done((bf16[2,512,256]{1,2,0:T(8,128)(2,1)}, bf16[2,512,256]{1,2,0:T(8,128)(2,1)}, u32[]{:S(2)}, u32[]{:S(2)}) %collective-permute-start.13) | collective-permute-done | bytes 524320 | tf_op jit(solution)/shard_map/ppermute | solution.py:18
  345.9 10.4 %collective-permute-done.14 = bf16[2,512,256]{1,2,0:T(8,128)(2,1)} collective-permute-done((bf16[2,512,256]{1,2,0:T(8,128)(2,1)}, bf16[2,512,256]{1,2,0:T(8,128)(2,1)}, u32[]{:S(2)}, u32[]{:S(2)}) %collective-permute-start.14) | collective-permute-done | bytes 524320 | tf_op jit(solution)/shard_map/ppermute | solution.py:18
  356.3 3.6 fusion.217
  360.0 3.0 collective-permute-start.15
  363.1 35.2 %collective-permute-done.15 = bf16[2,512,256]{1,2,0:T(8,128)(2,1)S(1)} collective-permute-done((bf16[2,512,256]{1,2,0:T(8,128)(2,1)}, bf16[2,512,256]{1,2,0:T(8,128)(2,1)S(1)}, u32[]{:S(2)}, u32[]{:S(2)}) %collective-permute-start.15) | collective-permute-done | bytes 524320 | tf_op jit(solution)/shard_map/ppermute | solution.py:18
  398.4 9.9 %collective-permute-done.16 = bf16[2,512,256]{1,2,0:T(8,128)(2,1)S(1)} collective-permute-done((bf16[2,512,256]{1,2,0:T(8,128)(2,1)}, bf16[2,512,256]{1,2,0:T(8,128)(2,1)S(1)}, u32[]{:S(2)}, u32[]{:S(2)}) %collective-permute-start.16) | collective-permute-done | bytes 524320 | tf_op jit(solution)/shard_map/ppermute | solution.py:18
  409.0 3.6 fusion.213
  414.8 12.9 %collective-permute-done.17 = bf16[2,512,256]{1,2,0:T(8,128)(2,1)S(1)} collective-permute-done((bf16[2,512,256]{1,2,0:T(8,128)(2,1)}, bf16[2,512,256]{1,2,0:T(8,128)(2,1)S(1)}, u32[]{:S(2)}, u32[]{:S(2)}) %collective-permute-start.17) | collective-permute-done | bytes 524320 | tf_op jit(solution)/shard_map/ppermute | solution.py:18
  427.7 9.1 %collective-permute-done.18 = bf16[2,512,256]{1,2,0:T(8,128)(2,1)} collective-permute-done((bf16[2,512,256]{1,2,0:T(8,128)(2,1)S(1)}, bf16[2,512,256]{1,2,0:T(8,128)(2,1)}, u32[]{:S(2)}, u32[]{:S(2)}) %collective-permute-start.18) | collective-permute-done | bytes 524320 | tf_op jit(solution)/shard_map/ppermute | solution.py:18
  436.8 3.6 fusion.209
  440.4 2.1 collective-permute-start.19
  442.5 1.4 collective-permute-start.20
  444.1 13.0 %collective-permute-done.19 = bf16[2,512,256]{1,2,0:T(8,128)(2,1)} collective-permute-done((bf16[2,512,256]{1,2,0:T(8,128)(2,1)}, bf16[2,512,256]{1,2,0:T(8,128)(2,1)}, u32[]{:S(2)}, u32[]{:S(2)}) %collective-permute-start.19) | collective-permute-done | bytes 524320 | tf_op jit(solution)/shard_map/ppermute | solution.py:18
  458.3 6.9 %collective-permute-done.20 = bf16[2,512,256]{1,2,0:T(8,128)(2,1)} collective-permute-done((bf16[2,512,256]{1,2,0:T(8,128)(2,1)}, bf16[2,512,256]{1,2,0:T(8,128)(2,1)}, u32[]{:S(2)}, u32[]{:S(2)}) %collective-permute-start.20) | collective-permute-done | bytes 524320 | tf_op jit(solution)/shard_map/ppermute | solution.py:18
  466.3 1.6 add_select_fusion.1
  468.0 5.1 convolution_convert_fusion
  473.1 134.7 %reduce-scatter.2.cloned.1.call-done = bf16[512,512]{1,0:T(8,128)(2,1)} async-done(((bf16[512,4096]{1,0:T(8,128)(2,1)}), bf16[512,512]{1,0:T(8,128)(2,1)}) %reduce-scatter.2.cloned.1.call-update) | async-done | bytes 524304 | tf_op jit(solution)/shard_map/reduce_scatter | solution.py:164
  (80 shorter events, 21.7 us)
Async XLA Ops:
  6.5 461.4 %copy-start = (bf16[256,4096]{1,0:T(8,128)(2,1)S(1)}, bf16[256,4096]{1,0:T(8,128)(2,1)}, u32[]{:S(2)}) copy-start(bf16[256,4096]{1,0:T(8,128)(2,1)} %param.15) | copy-start | bytes 6291460
  6.5 117.8 %all-gather.2.cloned.1.call-start = ((), (), s32[]{:S(2)}) async-start(), calls=%async_computation.1 | async-start | bytes 4718592 | tf_op jit(solution)/shard_map/all_gather | solution.py:86
  7.3 600.5 %reduce-scatter.2.cloned.1.call-start = ((), (), s32[]{:S(2)}) async-start(), calls=%async_computation.2 | async-start | bytes 4718592 | tf_op jit(solution)/shard_map/reduce_scatter | solution.py:164
  7.3 8.6 %copy-start.10 = (f32[3,3,256]{2,1,0:T(4,128)S(1)}, f32[3,3,256]{2,1,0:T(4,128)}, u32[]{:S(2)}) copy-start(f32[3,3,256]{2,1,0:T(4,128)} %param.11) | copy-start | bytes 27652
  7.3 8.7 %copy-start.8 = (f32[256,16]{0,1:T(8,128)S(1)}, f32[256,16]{0,1:T(8,128)}, u32[]{:S(2)}) copy-start(f32[256,16]{0,1:T(8,128)} %param.13) | copy-start | bytes 49156
  16.0 111.6 %copy-start.12 = (f32[4096]{0:T(1024)S(1)}, f32[4096]{0:T(1024)}, u32[]{:S(2)}) copy-start(f32[4096]{0:T(1024)} %param.9) | copy-start | bytes 49156
  124.3 3.4 copy-start.4
  134.0 0.9 copy-start.5
  135.2 9.7 %collective-permute-start = (bf16[2,3,256]{0,2,1:T(8,128)(2,1)S(1)}, bf16[2,3,256]{0,2,1:T(8,128)(2,1)S(1)}, u32[]{:S(2)}, u32[]{:S(2)}) collective-permute-start(bf16[2,3,256]{0,2,1:T(8,128)(2,1)S(1)} %bitcast.174), channel_id=1, source_target_pairs={{0,8},{8,16},{16,24},{24,32},{32,40},{40,48},{48,56},{56,64},{64,7... | collective-permute-start | bytes 9224 | tf_op jit(solution)/shard_map/ppermute | solution.py:14
  146.6 3.3 copy-start.2
  147.8 16.7 %collective-permute-start.1 = (bf16[2,512,256]{1,2,0:T(8,128)(2,1)}, bf16[2,512,256]{1,2,0:T(8,128)(2,1)}, u32[]{:S(2)}, u32[]{:S(2)}) collective-permute-start(bf16[2,512,256]{1,2,0:T(8,128)(2,1)} %fusion.112), channel_id=1, source_target_pairs={{0,128},{8,136},{16,144},{24,152},{32,160},{40,168},{48,176},{56,1... | collective-permute-start | bytes 1572872 | tf_op jit(solution)/shard_map/ppermute | solution.py:18
  149.9 1.0 copy-start.3
  150.9 19.4 %collective-permute-start.2 = (bf16[2,512,256]{1,2,0:T(8,128)(2,1)}, bf16[2,512,256]{1,2,0:T(8,128)(2,1)}, u32[]{:S(2)}, u32[]{:S(2)}) collective-permute-start(bf16[2,512,256]{1,2,0:T(8,128)(2,1)} %pad_convert_fusion), channel_id=1, source_target_pairs={{0,128},{8,136},{16,144},{24,152},{32,160},{40,168},{48,176},{56,1... | collective-permute-start | bytes 1572872 | tf_op jit(solution)/shard_map/ppermute | solution.py:18
  173.8 14.4 %collective-permute-start.3 = (bf16[2,512,256]{1,2,0:T(8,128)(2,1)}, bf16[2,512,256]{1,2,0:T(8,128)(2,1)S(1)}, u32[]{:S(2)}, u32[]{:S(2)}) collective-permute-start(bf16[2,512,256]{1,2,0:T(8,128)(2,1)} %get-tuple-element.40), channel_id=1, source_target_pairs={{0,64},{8,72},{16,80},{24,88},{32,96},{40,104},{48,112},{56,120},{... | collective-permute-start | bytes 1572872 | tf_op jit(solution)/shard_map/ppermute | solution.py:18
  174.3 19.4 %collective-permute-start.4 = (bf16[2,512,256]{1,2,0:T(8,128)(2,1)}, bf16[2,512,256]{1,2,0:T(8,128)(2,1)S(1)}, u32[]{:S(2)}, u32[]{:S(2)}) collective-permute-start(bf16[2,512,256]{1,2,0:T(8,128)(2,1)} %get-tuple-element.62), channel_id=1, source_target_pairs={{0,64},{8,72},{16,80},{24,88},{32,96},{40,104},{48,112},{56,120},{... | collective-permute-start | bytes 1572872 | tf_op jit(solution)/shard_map/ppermute | solution.py:18
  195.8 37.8 %collective-permute-start.5 = (bf16[2,512,256]{1,2,0:T(8,128)(2,1)S(1)}, bf16[2,512,256]{1,2,0:T(8,128)(2,1)S(1)}, u32[]{:S(2)}, u32[]{:S(2)}) collective-permute-start(bf16[2,512,256]{1,2,0:T(8,128)(2,1)S(1)} %get-tuple-element.36), channel_id=1, source_target_pairs={{0,32},{8,40},{16,48},{24,56},{32,0},{40,8},{48,16},{56,24},{64,96... | collective-permute-start | bytes 1572872 | tf_op jit(solution)/shard_map/ppermute | solution.py:18
  195.9 43.8 %collective-permute-start.6 = (bf16[2,512,256]{1,2,0:T(8,128)(2,1)S(1)}, bf16[2,512,256]{1,2,0:T(8,128)(2,1)S(1)}, u32[]{:S(2)}, u32[]{:S(2)}) collective-permute-start(bf16[2,512,256]{1,2,0:T(8,128)(2,1)S(1)} %get-tuple-element.60), channel_id=1, source_target_pairs={{0,32},{8,40},{16,48},{24,56},{32,0},{40,8},{48,16},{56,24},{64,96... | collective-permute-start | bytes 1572872 | tf_op jit(solution)/shard_map/ppermute | solution.py:18
  240.3 14.9 %collective-permute-start.7 = (bf16[2,512,256]{1,2,0:T(8,128)(2,1)S(1)}, bf16[2,512,256]{1,2,0:T(8,128)(2,1)S(1)}, u32[]{:S(2)}, u32[]{:S(2)}) collective-permute-start(bf16[2,512,256]{1,2,0:T(8,128)(2,1)S(1)} %get-tuple-element.32), channel_id=1, source_target_pairs={{0,16},{8,24},{16,0},{24,8},{32,48},{40,56},{48,32},{56,40},{64,80... | collective-permute-start | bytes 1572872 | tf_op jit(solution)/shard_map/ppermute | solution.py:18
  240.4 21.8 %collective-permute-start.8 = (bf16[2,512,256]{1,2,0:T(8,128)(2,1)S(1)}, bf16[2,512,256]{1,2,0:T(8,128)(2,1)S(1)}, u32[]{:S(2)}, u32[]{:S(2)}) collective-permute-start(bf16[2,512,256]{1,2,0:T(8,128)(2,1)S(1)} %get-tuple-element.58), channel_id=1, source_target_pairs={{0,16},{8,24},{16,0},{24,8},{32,48},{40,56},{48,32},{56,40},{64,80... | collective-permute-start | bytes 1572872 | tf_op jit(solution)/shard_map/ppermute | solution.py:18
  262.2 1.2 copy-start.9
  262.7 2.0 collective-permute-start.10
  262.8 2.6 collective-permute-start.9
  326.3 2.0 collective-permute-start.11
  326.5 2.5 collective-permute-start.12
  330.8 15.1 %collective-permute-start.13 = (bf16[2,512,256]{1,2,0:T(8,128)(2,1)}, bf16[2,512,256]{1,2,0:T(8,128)(2,1)}, u32[]{:S(2)}, u32[]{:S(2)}) collective-permute-start(bf16[2,512,256]{1,2,0:T(8,128)(2,1)} %get-tuple-element.52), channel_id=1, source_target_pairs={{0,16},{8,24},{16,0},{24,8},{32,48},{40,56},{48,32},{56,40},{64,80... | collective-permute-start | bytes 1572872 | tf_op jit(solution)/shard_map/ppermute | solution.py:18
  332.3 24.0 %collective-permute-start.14 = (bf16[2,512,256]{1,2,0:T(8,128)(2,1)}, bf16[2,512,256]{1,2,0:T(8,128)(2,1)}, u32[]{:S(2)}, u32[]{:S(2)}) collective-permute-start(bf16[2,512,256]{1,2,0:T(8,128)(2,1)} %get-tuple-element.17), channel_id=1, source_target_pairs={{0,16},{8,24},{16,0},{24,8},{32,48},{40,56},{48,32},{56,40},{64,80... | collective-permute-start | bytes 1572872 | tf_op jit(solution)/shard_map/ppermute | solution.py:18
  360.0 38.4 %collective-permute-start.15 = (bf16[2,512,256]{1,2,0:T(8,128)(2,1)}, bf16[2,512,256]{1,2,0:T(8,128)(2,1)S(1)}, u32[]{:S(2)}, u32[]{:S(2)}) collective-permute-start(bf16[2,512,256]{1,2,0:T(8,128)(2,1)} %get-tuple-element.50), channel_id=1, source_target_pairs={{0,32},{8,40},{16,48},{24,56},{32,0},{40,8},{48,16},{56,24},{64,96... | collective-permute-start | bytes 1572872 | tf_op jit(solution)/shard_map/ppermute | solution.py:18
  362.9 45.3 %collective-permute-start.16 = (bf16[2,512,256]{1,2,0:T(8,128)(2,1)}, bf16[2,512,256]{1,2,0:T(8,128)(2,1)S(1)}, u32[]{:S(2)}, u32[]{:S(2)}) collective-permute-start(bf16[2,512,256]{1,2,0:T(8,128)(2,1)} %get-tuple-element.13), channel_id=1, source_target_pairs={{0,32},{8,40},{16,48},{24,56},{32,0},{40,8},{48,16},{56,24},{64,96... | collective-permute-start | bytes 1572872 | tf_op jit(solution)/shard_map/ppermute | solution.py:18
  408.2 0.8 copy-start.7
  412.7 15.1 %collective-permute-start.17 = (bf16[2,512,256]{1,2,0:T(8,128)(2,1)}, bf16[2,512,256]{1,2,0:T(8,128)(2,1)S(1)}, u32[]{:S(2)}, u32[]{:S(2)}) collective-permute-start(bf16[2,512,256]{1,2,0:T(8,128)(2,1)} %get-tuple-element.48), channel_id=1, source_target_pairs={{0,64},{8,72},{16,80},{24,88},{32,96},{40,104},{48,112},{56,120},{... | collective-permute-start | bytes 1572872 | tf_op jit(solution)/shard_map/ppermute | solution.py:18
  413.8 23.0 %collective-permute-start.18 = (bf16[2,512,256]{1,2,0:T(8,128)(2,1)S(1)}, bf16[2,512,256]{1,2,0:T(8,128)(2,1)}, u32[]{:S(2)}, u32[]{:S(2)}) collective-permute-start(bf16[2,512,256]{1,2,0:T(8,128)(2,1)S(1)} %get-tuple-element.9), channel_id=1, source_target_pairs={{0,64},{8,72},{16,80},{24,88},{32,96},{40,104},{48,112},{56,120},{... | collective-permute-start | bytes 1572872 | tf_op jit(solution)/shard_map/ppermute | solution.py:18
  427.7 9.1 %copy-start.6 = (bf16[2,512,256]{1,2,0:T(8,128)(2,1)}, bf16[2,512,256]{1,2,0:T(8,128)(2,1)S(1)}, u32[]{:S(2)}) copy-start(bf16[2,512,256]{1,2,0:T(8,128)(2,1)S(1)} %collective-permute-done.17) | copy-start | bytes 1572868
  440.4 16.7 %collective-permute-start.19 = (bf16[2,512,256]{1,2,0:T(8,128)(2,1)}, bf16[2,512,256]{1,2,0:T(8,128)(2,1)}, u32[]{:S(2)}, u32[]{:S(2)}) collective-permute-start(bf16[2,512,256]{1,2,0:T(8,128)(2,1)} %get-tuple-element.46), channel_id=1, source_target_pairs={{0,128},{8,136},{16,144},{24,152},{32,160},{40,168},{48,176},{56,1... | collective-permute-start | bytes 1572872 | tf_op jit(solution)/shard_map/ppermute | solution.py:18
  442.5 22.6 %collective-permute-start.20 = (bf16[2,512,256]{1,2,0:T(8,128)(2,1)}, bf16[2,512,256]{1,2,0:T(8,128)(2,1)}, u32[]{:S(2)}, u32[]{:S(2)}) collective-permute-start(bf16[2,512,256]{1,2,0:T(8,128)(2,1)} %get-tuple-element.5), channel_id=1, source_target_pairs={{0,128},{8,136},{16,144},{24,152},{32,160},{40,168},{48,176},{56,1... | collective-permute-start | bytes 1572872 | tf_op jit(solution)/shard_map/ppermute | solution.py:18
  444.1 22.2 %copy-start.1 = (f32[2,512,256]{1,2,0:T(8,128)S(1)}, f32[2,512,256]{1,2,0:T(8,128)}, u32[]{:S(2)}) copy-start(f32[2,512,256]{1,2,0:T(8,128)} %get-tuple-element.47) | copy-start | bytes 3145732
  466.3 1.6 copy-start.11
Sparse Core Ops, SparseCore 0:
  9.8 114.4 all-gather.1
  473.2 134.5 reduce-scatter.1
where the time goes:
time: 624 us; the launch traced here: 615 us
  waiting for transfers between devices  449 us (72%)
  matrix products  71.2 us (11%)
  starting transfers between devices  35.1 us (6%)
  other arithmetic  30.7 us (5%)
  between operations  15.6 us (2%)
  local copies, waits for them, and re-layouts  13.1 us (2%)
    ppermute x20, waiting for transfers between devices, swapped(): lax.ppermute(array, axis, [(i, i ^ 1 << distance) for i in range(lax.axis...  199 us
    reduce_scatter x1, waiting for transfers between devices, local(): lax.psum_scatter(terms.astype(jnp.bfloat16), 'tp', scatter_dimension=1, t...  135 us
    all_gather x1, waiting for transfers between devices, local(): whole_rows = lax.all_gather(tokens, 'tp', axis=1, tiled=True)  108 us
    dot_general x8, matrix products, contract(): return jnp.einsum(form, table, values, precision=precise)  59.9 us
    ppermute x20, starting transfers between devices, swapped(): lax.ppermute(array, axis, [(i, i ^ 1 << distance) for i in range(lax.axis...  33.1 us
    convert_element_type x4, other arithmetic, local(): imag_part.astype(jnp.bfloat16)  12.6 us
  transfers between devices with their start and end apart: 23, of which 23 were waited for; matrix products, arithmetic and copies ran while one was open for 2% of the time, Pallas kernels for 0%

commit v1 on v0

v1 whole, which is shorter than its diff:
```python
import jax
import jax.numpy as jnp
from jax import lax
from jax.experimental import pallas as pl
from jax.experimental.pallas import tpu as pltpu
from jax.sharding import PartitionSpec as P

MESH = pl.DeviceIdType.MESH
F32 = jnp.float32
BF16 = jnp.bfloat16

X, ZL, CORES = 4, 4, 2
ZH, Y = 2, 4
N_CTX = X * ZL * CORES
N_TP = ZH * Y
ROWS = 512
FEAT = 512
D = 4096
CHL = 256
MODES = 16
PIECES = 4
PROWS = ROWS // PIECES
HALF = PROWS // 2
HALO = 16
EXT = ROWS + HALO
T = 16
NCH = ROWS // T
LANES = 128
HV = CHL // LANES


def remote(src, dst, send, recv, device):
    return pltpu.make_async_remote_copy(
        src_ref=src, dst_ref=dst, send_sem=send, recv_sem=recv, device_id=device, device_id_type=MESH
    )


def kernel(
    tok, gain, w_in, w_short, res, dec, direct, w_out, out,
    xg, halo, wv, xs, ssq, acc, pb, qb, xb, yb, ft, ab, eb, sb, gb, own, gg, wo, oacc,
    st_core, st_z, st_x,
    s1, r1, s2, r2, hs, hr, ws, wr, zs, zr, xsnd, xrcv, cs, cr, es, er, lsem,
):
    ctx = lax.axis_index("ctx")
    tp = lax.axis_index("tp")
    x, zl, core = ctx // (ZL * CORES), (ctx // CORES) % ZL, ctx % CORES
    zh, y = tp // Y, tp % Y

    def at_ctx(xx, zz, cc):
        return ((xx * ZL + zz) * CORES + cc, tp)

    def at_tp(hh, yy):
        return (ctx, hh * Y + yy)

    right, left = at_tp(zh, (y + 1) % Y), at_tp(zh, (y + Y - 1) % Y)
    across = at_tp(1 - zh, y)
    tp_others = [(a, b) for a in range(ZH) for b in range(Y) if a or b]
    tp_dev = [at_tp((zh + a) % ZH, (y + b) % Y) for a, b in tp_others]
    z_dev = [at_ctx(x, (zl + b) % ZL, core) for b in range(1, ZL)]
    x_dev = [at_ctx((x + a) % X, zl, core) for a in range(1, X)]
    other = at_ctx(x, zl, 1 - core)
    after = ((ctx + 1) % N_CTX, tp)
    before = ((ctx + N_CTX - 1) % N_CTX, tp)

    w_load = pltpu.make_async_copy(w_in, wv, lsem.at[0])
    w_load.start()

    barrier = pltpu.get_barrier_semaphore()
    greeted = tp_dev + z_dev + x_dev + [other, after, before]
    for device in greeted:
        pl.semaphore_signal(barrier, inc=1, device_id=device, device_id_type=MESH)
    pl.semaphore_wait(barrier, len(greeted))

    def rows_of(c, half=None):
        start = ROWS - PROWS * (c + 1)
        if half is None:
            return pl.ds(start, PROWS)
        return pl.ds(start + half * HALF, HALF)

    class Gather:
        def __init__(self, mine, buf, send, recv):
            self.mine, self.buf, self.send, self.recv = mine, buf, send, recv

        def held(self, p, s):
            return self.mine if (p, s) == (0, 0) else self.buf.at[p, s]

        def copy(self, kind, p, c):
            if kind == 0:
                src, dst, dev = self.held(p, 0).at[rows_of(c)], self.buf.at[p, 1, rows_of(c)], right
            elif kind == 1:
                src, dst, dev = self.held(p, 0).at[rows_of(c)], self.buf.at[p, 3, rows_of(c)], left
            elif kind == 2:
                src, dst, dev = self.buf.at[p, 1, rows_of(c, 0)], self.buf.at[p, 2, rows_of(c, 0)], right
            elif kind == 3:
                src, dst, dev = self.buf.at[p, 3, rows_of(c, 1)], self.buf.at[p, 2, rows_of(c, 1)], left
            else:
                src, dst, dev = self.mine.at[rows_of(c)], self.buf.at[1, 0, rows_of(c)], across
            return remote(src, dst, self.send.at[kind, p, c], self.recv.at[kind, p, c], dev)

        def cross(self):
            for c in range(PIECES):
                self.copy(4, 0, c).start()

        def spread(self, p, c):
            if p == 1:
                self.copy(4, 0, c).wait_recv()
            self.copy(0, p, c).start()
            self.copy(1, p, c).start()

        def forward(self, p, c):
            self.copy(0, p, c).wait_recv()
            self.copy(2, p, c).start()
            self.copy(1, p, c).wait_recv()
            self.copy(3, p, c).start()

        def arrive(self, p, c):
            self.copy(2, p, c).wait_recv()
            self.copy(3, p, c).wait_recv()

        def sent(self):
            for c in range(PIECES):
                self.copy(4, 0, c).wait_send()
                for p in range(2):
                    for kind in range(4):
                        self.copy(kind, p, c).wait_send()

    def owner(p, s):
        return (zh + p) % ZH * Y + (y + (0, Y - 1, 2, 1)[s]) % Y

    tokens = Gather(tok, xg, s1, r1)

    def halo_copy(p, s):
        return remote(
            tokens.held(p, s).at[pl.ds(ROWS - HALO, HALO)], halo.at[p, s], hs.at[p, s], hr.at[p, s], after
        )

    chip = x * ZL + zl
    lane0 = pl.multiple_of(core * CHL, CHL)

    def wo_first(i):
        a, b = tp_others[i]
        dev = tp_dev[i]
        col = pl.multiple_of(dev[1] * FEAT + core * CHL, CHL)
        rows = pl.ds(pl.multiple_of(chip * HALO, HALO), HALO)
        return remote(
            w_out.at[rows, pl.ds(col, CHL)], wo.at[tp, rows, pl.ds(lane0, CHL)], ws.at[i], wr.at[i], dev
        )

    def wo_mine():
        col = pl.multiple_of(tp * FEAT + core * CHL, CHL)
        rows = pl.ds(pl.multiple_of(chip * HALO, HALO), HALO)
        return pltpu.make_async_copy(w_out.at[rows, pl.ds(col, CHL)], wo.at[tp, rows, pl.ds(lane0, CHL)], lsem.at[1])

    def wo_z(i):
        part = wo.at[:, pl.ds(pl.multiple_of(chip * HALO, HALO), HALO), pl.ds(lane0, CHL)]
        return remote(part, part, zs.at[i], zr.at[i], z_dev[i])

    def wo_x(i):
        part = wo.at[:, pl.ds(pl.multiple_of(x * ZL * HALO, ZL * HALO), ZL * HALO), pl.ds(lane0, CHL)]
        return remote(part, part, xsnd.at[i], xrcv.at[i], x_dev[i])

    def wo_core():
        part = wo.at[:, :, pl.ds(lane0, CHL)]
        return remote(part, part, cs.at[0], cr.at[0], other)

    def project(p, s):
        halo_copy(p, s).wait_recv()
        k = owner(p, s)
        block = tokens.held(p, s)
        scale = jnp.concatenate([gain[pl.ds(4 * k + i, 1), :] for i in range(4)], axis=1)
        head = halo[p, s].astype(F32)
        xs[0:HALO, :] = (head * scale).astype(BF16)
        ssq[0:HALO, :] += sum(jnp.square(head[:, LANES * i:LANES * (i + 1)]) for i in range(4))

        @pl.loop(0, ROWS // 64)
        def _(i):
            at = pl.ds(pl.multiple_of(i * 64, 64), 64)
            to = pl.ds(pl.multiple_of(i * 64 + HALO, HALO), 64)
            values = block[at, :].astype(F32)
            xs[to, :] = (values * scale).astype(BF16)
            ssq[to, :] += sum(jnp.square(values[:, LANES * j:LANES * (j + 1)]) for j in range(4))

        @pl.loop(0, 3)
        def _(g):
            weights = wv[g, pl.ds(pl.multiple_of(k * FEAT, FEAT), FEAT), :]
            acc[g] += jnp.dot(xs[...], weights, preferred_element_type=F32)

    tokens.cross()
    for c in range(PIECES):
        tokens.spread(0, c)
    halo_copy(0, 0).start()
    for i in range(N_TP - 1):
        wo_first(i).start()
    wo_mine().start()

    ssq[...] = jnp.zeros_like(ssq)
    acc[...] = jnp.zeros_like(acc)
    rate = dec[...]
    weight = res[...]
    powers = []
    for lag in range(T):
        row = jnp.sum(weight * jnp.exp(-rate * float(lag)), axis=0, keepdims=True)
        if lag == 0:
            row = row + direct[...]
        for h in range(HV):
            ft[h, lag:lag + 1, :] = row[:, LANES * h:LANES * (h + 1)]
    decay1 = jnp.exp(-rate)
    for h in range(HV):
        ab[h] = decay1[:, LANES * h:LANES * (h + 1)]

    tokens.forward(0, 0)
    halo_copy(0, 1).start()
    halo_copy(0, 3).start()
    w_load.wait()
    project(0, 0)
    tokens.forward(0, 1)
    wo_mine().wait()
    for i in range(N_TP - 1):
        wo_first(i).wait_recv()
    for i in range(ZL - 1):
        wo_z(i).start()
    tokens.spread(1, 0)
    halo_copy(1, 0).start()
    tokens.forward(0, 2)
    tokens.forward(0, 3)
    tokens.arrive(0, 0)
    halo_copy(0, 2).start()
    project(0, 1)
    tokens.spread(1, 1)
    project(0, 3)
    for i in range(ZL - 1):
        wo_z(i).wait_recv()
    for i in range(X - 1):
        wo_x(i).start()
    for c in range(1, PIECES):
        tokens.arrive(0, c)
    tokens.forward(1, 0)
    halo_copy(1, 1).start()
    halo_copy(1, 3).start()
    tokens.spread(1, 2)
    project(0, 2)
    tokens.forward(1, 1)
    tokens.arrive(1, 0)
    halo_copy(1, 2).start()
    tokens.spread(1, 3)
    project(1, 0)
    for i in range(X - 1):
        wo_x(i).wait_recv()
    wo_core().start()
    tokens.forward(1, 2)
    tokens.forward(1, 3)
    project(1, 1)
    project(1, 3)
    for c in range(1, PIECES):
        tokens.arrive(1, c)
    project(1, 2)

    inverse = lax.rsqrt(jnp.sum(ssq[...], axis=1, keepdims=True) * (1.0 / D) + 1e-06)
    row_id = lax.broadcasted_iota(jnp.int32, (EXT, 1), 0)
    inverse = jnp.where((row_id < HALO) & (ctx == 0), 0.0, inverse)
    for g in range(3):
        for h in range(HV):
            pb[g, h] = (acc[g, :, LANES * h:LANES * (h + 1)] * inverse).astype(BF16).astype(F32)

    for h in range(HV):
        lanes = pl.ds(LANES * h, LANES)

        @pl.loop(0, T)
        def _(t):
            streams = []
            for g in range(3):
                total = None
                for j in range(3):
                    plane = pb[g, h, pl.ds(HALO + t - j, NCH, stride=T), :]
                    term = w_short[j, pl.ds(g, 1), lanes] * plane
                    total = term if total is None else total + term
                streams.append(total)
            qb[h, t] = streams[0]
            xb[h, t] = streams[1] * streams[2]

    group = 4
    for h in range(HV):
        for r0 in range(0, MODES, group):
            factors = [jnp.broadcast_to(ab[h, r:r + 1, :], (NCH, LANES)) for r in range(r0, r0 + group)]

            def step(t, states):
                value = xb[h, t]
                return tuple(f * s + value for f, s in zip(factors, states))

            states = lax.fori_loop(0, T, step, tuple(jnp.zeros((NCH, LANES), F32) for _ in factors))
            for i, s in enumerate(states):
                eb[h, (r0 + i) * NCH:(r0 + i + 1) * NCH, :] = s

    block_end = []
    for h in range(HV):
        chunk_decay = jnp.exp(-dec[:, LANES * h:LANES * (h + 1)] * float(T))

        def scan(n, state):
            sb[h, pl.ds(pl.multiple_of(n * MODES, MODES), MODES), :] = state
            return chunk_decay * state + eb[h, pl.ds(n, MODES, stride=NCH), :]

        block_end.append(lax.fori_loop(0, NCH, scan, jnp.zeros((MODES, LANES), F32)))
    mine = jnp.concatenate(block_end, axis=1)

    st_core[0] = mine
    core_copy = remote(st_core.at[0], st_core.at[1], es.at[0], er.at[0], other)
    core_copy.start()
    decay_block = jnp.exp(-dec[...] * float(ROWS))
    decay_chip = jnp.exp(-dec[...] * float(ROWS * CORES))
    decay_line = jnp.exp(-dec[...] * float(ROWS * CORES * ZL))
    core_copy.wait_recv()
    theirs = st_core[1]
    st_z[0] = jnp.where(core == 0, decay_block * mine + theirs, decay_block * theirs + mine)
    z_copies = [
        remote(st_z.at[0], st_z.at[b], es.at[b], er.at[b], z_dev[b - 1]) for b in range(1, ZL)
    ]
    for copy in z_copies:
        copy.start()

    def within(h):
        for t in range(T):
            total = None
            for lag in range(t + 1):
                term = ft[h, lag:lag + 1, :] * xb[h, t - lag]
                total = term if total is None else total + term
            yb[h, t] = total

    within(0)
    for copy in z_copies:
        copy.wait_recv()
    line_end = jnp.zeros((MODES, CHL), F32)
    chip_in = jnp.zeros((MODES, CHL), F32)
    for zz in range(ZL):
        for b in range(ZL):
            here = (zl + ZL - b) % ZL == zz
            piece = st_z[b]
            if b == 0:
                chosen = jnp.where(here, piece, 0.0)
            else:
                chosen = jnp.where(here, piece, chosen)
        line_end = decay_chip * line_end + chosen
        chip_in = jnp.where(zz < zl, decay_chip * chip_in + chosen, chip_in)
    st_x[0] = line_end
    x_copies = [
        remote(st_x.at[0], st_x.at[a], es.at[ZL + a - 1], er.at[ZL + a - 1], x_dev[a - 1]) for a in range(1, X)
    ]
    for copy in x_copies:
        copy.start()
    within(1)
    before_chip = jnp.exp(-dec[...] * (ROWS * CORES * zl).astype(F32))
    for copy in x_copies:
        copy.wait_recv()
    line_in = jnp.zeros((MODES, CHL), F32)
    for xx in range(X):
        for a in range(X):
            here = (x + X - a) % X == xx
            piece = st_x[a]
            if a == 0:
                chosen = jnp.where(here, piece, 0.0)
            else:
                chosen = jnp.where(here, piece, chosen)
        line_in = jnp.where(xx < x, decay_line * line_in + chosen, line_in)
    chip_in = chip_in + before_chip * line_in
    carried = jnp.where(core == 0, chip_in, decay_block * chip_in + theirs)

    for h in range(HV):
        part = slice(LANES * h, LANES * (h + 1))
        chunk_decay = jnp.exp(-dec[:, part] * float(T))
        front = res[:, part] * ab[h]

        def enter(n, state):
            at = pl.ds(pl.multiple_of(n * MODES, MODES), MODES)
            sb[h, at, :] = front * (sb[h, at, :] + state)
            return chunk_decay * state

        lax.fori_loop(0, NCH, enter, carried[:, part])
        for r0 in range(0, MODES, group):
            factors = [jnp.broadcast_to(ab[h, r:r + 1, :], (NCH, LANES)) for r in range(r0, r0 + group)]
            start = tuple(sb[h, pl.ds(r, NCH, stride=MODES), :] for r in range(r0, r0 + group))
            last = r0 + group == MODES

            def step(t, terms):
                total = yb[h, t] + sum(terms[1:], terms[0])
                if last:
                    gb[h, pl.ds(t, NCH, stride=T), :] = qb[h, t] * total
                else:
                    yb[h, t] = total
                return tuple(f * s for f, s in zip(factors, terms))

            lax.fori_loop(0, T, step, start)
    for h in range(HV):
        own[:, LANES * h:LANES * (h + 1)] = gb[h].astype(BF16)

    gates = Gather(own, gg, s2, r2)

    def emit(p, s, first=False, last=False):
        weights = wo[owner(p, s)]
        value = jnp.dot(gates.held(p, s)[...], weights, preferred_element_type=F32)
        if first:
            oacc[...] = value
        elif last:
            out[...] = (oacc[...] + value).astype(BF16)
        else:
            oacc[...] += value

    gates.cross()
    for c in range(PIECES):
        gates.spread(0, c)
    wo_core().wait_recv()
    emit(0, 0, first=True)
    for c in range(PIECES):
        gates.forward(0, c)
        if c >= 2:
            gates.spread(1, c - 2)
    emit(0, 1)
    emit(0, 3)
    for c in range(PIECES):
        gates.arrive(0, c)
    gates.spread(1, 2)
    emit(0, 2)
    gates.forward(1, 0)
    gates.spread(1, 3)
    emit(1, 0)
    for c in range(1, PIECES):
        gates.forward(1, c)
    emit(1, 1)
    emit(1, 3)
    for c in range(PIECES):
        gates.arrive(1, c)
    emit(1, 2, last=True)

    tokens.sent()
    gates.sent()
    for p in range(ZH):
        for s in range(Y):
            halo_copy(p, s).wait_send()
    for i in range(N_TP - 1):
        wo_first(i).wait_send()
    for i in range(ZL - 1):
        wo_z(i).wait_send()
    for i in range(X - 1):
        wo_x(i).wait_send()
    wo_core().wait_send()
    core_copy.wait_send()
    for copy in z_copies + x_copies:
        copy.wait_send()


def local(tokens, norm_gain, w_in, w_short, residues, decays, direct, w_out):
    dma = pltpu.SemaphoreType.DMA
    vmem = pl.BlockSpec(memory_space=pltpu.VMEM)
    hbm = pl.BlockSpec(memory_space=pl.ANY)
    return pl.pallas_call(
        kernel,
        out_shape=jax.ShapeDtypeStruct((ROWS, FEAT), BF16),
        in_specs=[vmem, vmem, hbm, vmem, vmem, vmem, vmem, hbm],
        out_specs=vmem,
        scratch_shapes=[
            pltpu.VMEM((ZH, Y, ROWS, FEAT), BF16),
            pltpu.VMEM((ZH, Y, HALO, FEAT), BF16),
            pltpu.VMEM((3, D, CHL), BF16),
            pltpu.VMEM((EXT, FEAT), BF16),
            pltpu.VMEM((EXT, LANES), F32),
            pltpu.VMEM((3, EXT, CHL), F32),
            pltpu.VMEM((3, HV, EXT, LANES), F32),
            pltpu.VMEM((HV, T, NCH, LANES), F32),
            pltpu.VMEM((HV, T, NCH, LANES), F32),
            pltpu.VMEM((HV, T, NCH, LANES), F32),
            pltpu.VMEM((HV, T, LANES), F32),
            pltpu.VMEM((HV, MODES, LANES), F32),
            pltpu.VMEM((HV, MODES * NCH, LANES), F32),
            pltpu.VMEM((HV, MODES * NCH, LANES), F32),
            pltpu.VMEM((HV, ROWS, LANES), F32),
            pltpu.VMEM((ROWS, CHL), BF16),
            pltpu.VMEM((ZH, Y, ROWS, CHL), BF16),
            pltpu.VMEM((N_TP, CHL, FEAT), BF16),
            pltpu.VMEM((ROWS, FEAT), F32),
            pltpu.VMEM((2, MODES, CHL), F32),
            pltpu.VMEM((ZL, MODES, CHL), F32),
            pltpu.VMEM((X, MODES, CHL), F32),
            dma((5, 2, PIECES)), dma((5, 2, PIECES)),
            dma((5, 2, PIECES)), dma((5, 2, PIECES)),
            dma((ZH, Y)), dma((ZH, Y)),
            dma((N_TP - 1,)), dma((N_TP - 1,)),
            dma((ZL - 1,)), dma((ZL - 1,)),
            dma((X - 1,)), dma((X - 1,)),
            dma((1,)), dma((1,)),
            dma((ZL + X - 1,)), dma((ZL + X - 1,)),
            dma((2,)),
        ],
        compiler_params=pltpu.CompilerParams(
            collective_id=0, has_side_effects=True, vmem_limit_bytes=56 * 1024 * 1024
        ),
        name="hyena",
    )(
        tokens,
        norm_gain.reshape(D // LANES, LANES),
        w_in.transpose(1, 0, 2),
        w_short,
        residues.T,
        decays.T,
        direct.reshape(1, CHL),
        w_out,
    )


def solution(mesh):
    placed = (
        P("ctx", "tp"),
        P(),
        P(None, None, "tp"),
        P(None, None, "tp"),
        P("tp", None),
        P("tp", None),
        P("tp"),
        P("tp", None),
    )
    return jax.shard_map(local, mesh=mesh, in_specs=placed, out_specs=P("ctx", "tp"), check_vma=False)
```

time: 624 us -> 105 us (0.17)
  the two profiles are of different devices: /device:TPU:2 before, /device:TPU:76 now
where the time goes in v1:
time: 105 us
  Pallas kernels  103 us (98%)
  local copies, waits for them, and re-layouts  1.87 us (2%)
    pallas_call x1, Pallas kernels, local(): pl.pallas_call(kernel, out_shape=jax.ShapeDtypeStruct((ROWS, FEAT), BF16)...  103 us

profile of v1, /device:TPU:76, one launch (start us, length us, event | category | flops | bytes accessed | tf_op | source)
XLA Modules:
  0.0 104.9 jit_solution(1618453788108784027)
XLA Ops:
  0.0 103.1 %hyena.1 = bf16[512,512]{1,0:T(8,128)(2,1)} custom-call(bf16[512,512]{1,0:T(8,128)(2,1)} %tok.1, f32[32,128]{1,0:T(8,128)} %bitcast.6, bf16[3,4096,256]{2,1,0:T(8,128)(2,1)} %bitcast.5, f32[3,3,256]{2,1,0:T(4,128)} %w_short.1, f32[16,256]{1,0:T(8,128)} %bitcast.7, f32[16,256]{1,0:T(8,128)} %bitcast.8, f32[1,256]{1,0:T(1,128)} %bitcast.9, bf16[256,4096]{1,0:T(8,128)(2,1)} %w_out.1), custom_call_target="tpu_custom_call" | custom-call | tf_op jit(solution)/shard_map/hyena/pallas_call | solution.py:453
  103.1 1.9 %copy.10 = bf16[512,512]{1,0:T(8,128)(2,1)} copy(bf16[512,512]{1,0:T(8,128)(2,1)} %hyena.1) | data formatting | bytes 1048576

commit v2 on v1

--- a/solution.py
+++ b/solution.py
@@ -22,6 +22,7 @@
 PROWS = ROWS // PIECES
 HALF = PROWS // 2
 HALO = 16
+WINDOW = 2
 EXT = ROWS + HALO
 T = 16
 NCH = ROWS // T
@@ -37,8 +38,8 @@
 
 def kernel(
     tok, gain, w_in, w_short, res, dec, direct, w_out, out,
-    xg, halo, wv, xs, ssq, acc, pb, qb, xb, yb, ft, ab, eb, sb, gb, own, gg, wo, oacc,
-    st_core, st_z, st_x,
+    xg, halo, wv, xs, ssq, acc, pb, qb, xb, yb, ft, ab, eb, sb, pw, gb, own, gg, wo, wt, oacc,
+    st_core, st_z, st_x, st_in,
     s1, r1, s2, r2, hs, hr, ws, wr, zs, zr, xsnd, xrcv, cs, cr, es, er, lsem,
 ):
     ctx = lax.axis_index("ctx")
@@ -54,8 +55,7 @@
 
     right, left = at_tp(zh, (y + 1) % Y), at_tp(zh, (y + Y - 1) % Y)
     across = at_tp(1 - zh, y)
-    tp_others = [(a, b) for a in range(ZH) for b in range(Y) if a or b]
-    tp_dev = [at_tp((zh + a) % ZH, (y + b) % Y) for a, b in tp_others]
+    y_dev = [at_tp(zh, (y + b) % Y) for b in range(1, Y)]
     z_dev = [at_ctx(x, (zl + b) % ZL, core) for b in range(1, ZL)]
     x_dev = [at_ctx((x + a) % X, zl, core) for a in range(1, X)]
     other = at_ctx(x, zl, 1 - core)
@@ -66,7 +66,7 @@
     w_load.start()
 
     barrier = pltpu.get_barrier_semaphore()
-    greeted = tp_dev + z_dev + x_dev + [other, after, before]
+    greeted = y_dev + z_dev + x_dev + [across, other, after, before]
     for device in greeted:
         pl.semaphore_signal(barrier, inc=1, device_id=device, device_id_type=MESH)
     pl.semaphore_wait(barrier, len(greeted))
@@ -80,6 +80,7 @@
     class Gather:
         def __init__(self, mine, buf, send, recv):
             self.mine, self.buf, self.send, self.recv = mine, buf, send, recv
+            self.queue = []
 
         def held(self, p, s):
             return self.mine if (p, s) == (0, 0) else self.buf.at[p, s]
@@ -97,32 +98,38 @@
                 src, dst, dev = self.mine.at[rows_of(c)], self.buf.at[1, 0, rows_of(c)], across
             return remote(src, dst, self.send.at[kind, p, c], self.recv.at[kind, p, c], dev)
 
-        def cross(self):
-            for c in range(PIECES):
-                self.copy(4, 0, c).start()
+        def push(self, *copies):
+            if len(self.queue) >= WINDOW:
+                for copy in self.queue[-WINDOW]:
+                    copy.wait_send()
+            for copy in copies:
+                copy.start()
+            self.queue.append(copies)
+
+        def cross(self, c):
+            if c:
+                self.copy(4, 0, c - 1).wait_send()
+            self.copy(4, 0, c).start()
 
         def spread(self, p, c):
             if p == 1:
                 self.copy(4, 0, c).wait_recv()
-            self.copy(0, p, c).start()
-            self.copy(1, p, c).start()
+            self.push(self.copy(0, p, c), self.copy(1, p, c))
 
         def forward(self, p, c):
             self.copy(0, p, c).wait_recv()
-            self.copy(2, p, c).start()
             self.copy(1, p, c).wait_recv()
-            self.copy(3, p, c).start()
+            self.push(self.copy(2, p, c), self.copy(3, p, c))
 
         def arrive(self, p, c):
             self.copy(2, p, c).wait_recv()
             self.copy(3, p, c).wait_recv()
 
         def sent(self):
-            for c in range(PIECES):
-                self.copy(4, 0, c).wait_send()
-                for p in range(2):
-                    for kind in range(4):
-                        self.copy(kind, p, c).wait_send()
+            self.copy(4, 0, PIECES - 1).wait_send()
+            for copies in self.queue[-WINDOW:]:
+                for copy in copies:
+                    copy.wait_send()
 
     def owner(p, s):
         return (zh + p) % ZH * Y + (y + (0, Y - 1, 2, 1)[s]) % Y
@@ -137,30 +144,38 @@
     chip = x * ZL + zl
     lane0 = pl.multiple_of(core * CHL, CHL)
 
-    def wo_first(i):
-        a, b = tp_others[i]
-        dev = tp_dev[i]
-        col = pl.multiple_of(dev[1] * FEAT + core * CHL, CHL)
-        rows = pl.ds(pl.multiple_of(chip * HALO, HALO), HALO)
-        return remote(
-            w_out.at[rows, pl.ds(col, CHL)], wo.at[tp, rows, pl.ds(lane0, CHL)], ws.at[i], wr.at[i], dev
-        )
+    wo_rows = pl.ds(pl.multiple_of(chip * HALO, HALO), HALO)
+    wo_lanes = pl.ds(lane0, CHL)
+
+    def wo_columns(device):
+        return w_out.at[wo_rows, pl.ds(pl.multiple_of(device[1] * FEAT + core * CHL, CHL), CHL)]
+
+    def wo_across(b):
+        dst = wt.at[b - 1] if b else wo.at[tp, wo_rows, wo_lanes]
+        return remote(wo_columns(at_tp(1 - zh, (y + b) % Y)), dst, ws.at[b], wr.at[b], across)
+
+    def wo_y(b):
+        dst = wo.at[tp, wo_rows, wo_lanes]
+        return remote(wo_columns(y_dev[b - 1]), dst, ws.at[Y + b - 1], wr.at[Y + b - 1], y_dev[b - 1])
+
+    def wo_relayed(b):
+        dst = wo.at[across[1], wo_rows, wo_lanes]
+        at = 2 * Y + b - 2
+        return remote(wt.at[b - 1], dst, ws.at[at], wr.at[at], y_dev[b - 1])
 
     def wo_mine():
-        col = pl.multiple_of(tp * FEAT + core * CHL, CHL)
-        rows = pl.ds(pl.multiple_of(chip * HALO, HALO), HALO)
-        return pltpu.make_async_copy(w_out.at[rows, pl.ds(col, CHL)], wo.at[tp, rows, pl.ds(lane0, CHL)], lsem.at[1])
+        return pltpu.make_async_copy(wo_columns((ctx, tp)), wo.at[tp, wo_rows, wo_lanes], lsem.at[1])
 
     def wo_z(i):
-        part = wo.at[:, pl.ds(pl.multiple_of(chip * HALO, HALO), HALO), pl.ds(lane0, CHL)]
+        part = wo.at[:, wo_rows, wo_lanes]
         return remote(part, part, zs.at[i], zr.at[i], z_dev[i])
 
     def wo_x(i):
-        part = wo.at[:, pl.ds(pl.multiple_of(x * ZL * HALO, ZL * HALO), ZL * HALO), pl.ds(lane0, CHL)]
+        part = wo.at[:, pl.ds(pl.multiple_of(x * ZL * HALO, ZL * HALO), ZL * HALO), wo_lanes]
         return remote(part, part, xsnd.at[i], xrcv.at[i], x_dev[i])
 
     def wo_core():
-        part = wo.at[:, :, pl.ds(lane0, CHL)]
+        part = wo.at[:, :, wo_lanes]
         return remote(part, part, cs.at[0], cr.at[0], other)
 
     def project(p, s):
@@ -185,12 +200,14 @@
             weights = wv[g, pl.ds(pl.multiple_of(k * FEAT, FEAT), FEAT), :]
             acc[g] += jnp.dot(xs[...], weights, preferred_element_type=F32)
 
-    tokens.cross()
-    for c in range(PIECES):
-        tokens.spread(0, c)
+    tokens.cross(0)
+    tokens.spread(0, 0)
+    tokens.spread(0, 1)
     halo_copy(0, 0).start()
-    for i in range(N_TP - 1):
-        wo_first(i).start()
+    for b in range(Y):
+        wo_across(b).start()
+    for b in range(1, Y):
+        wo_y(b).start()
     wo_mine().start()
 
     ssq[...] = jnp.zeros_like(ssq)
@@ -208,45 +225,59 @@
     for h in range(HV):
         ab[h] = decay1[:, LANES * h:LANES * (h + 1)]
 
+    @pl.loop(0, NCH)
+    def _(n):
+        table = res[...] * jnp.exp(-dec[...] * (T * n + 1).astype(F32))
+        for h in range(HV):
+            pw[h, pl.ds(pl.multiple_of(n * MODES, MODES), MODES), :] = table[:, LANES * h:LANES * (h + 1)]
+
+
+    tokens.spread(0, 2)
     tokens.forward(0, 0)
     halo_copy(0, 1).start()
     halo_copy(0, 3).start()
+    tokens.cross(1)
     w_load.wait()
     project(0, 0)
+    tokens.spread(0, 3)
     tokens.forward(0, 1)
+    tokens.arrive(0, 0)
+    halo_copy(0, 2).start()
+    tokens.cross(2)
+    tokens.forward(0, 2)
+    for b in range(1, Y):
+        wo_across(b).wait_recv()
+        wo_relayed(b).start()
+    tokens.forward(0, 3)
+    tokens.spread(1, 0)
+    halo_copy(1, 0).start()
+    project(0, 1)
+    tokens.spread(1, 1)
+    tokens.cross(3)
+    project(0, 3)
+    for c in range(1, PIECES):
+        tokens.arrive(0, c)
+    project(0, 2)
+    tokens.forward(1, 0)
+    halo_copy(1, 1).start()
+    halo_copy(1, 3).start()
+    tokens.spread(1, 2)
     wo_mine().wait()
-    for i in range(N_TP - 1):
-        wo_first(i).wait_recv()
+    wo_across(0).wait_recv()
+    for b in range(1, Y):
+        wo_y(b).wait_recv()
+        wo_relayed(b).wait_recv()
     for i in range(ZL - 1):
         wo_z(i).start()
-    tokens.spread(1, 0)
-    halo_copy(1, 0).start()
-    tokens.forward(0, 2)
-    tokens.forward(0, 3)
-    tokens.arrive(0, 0)
-    halo_copy(0, 2).start()
-    project(0, 1)
-    tokens.spread(1, 1)
-    project(0, 3)
+    tokens.forward(1, 1)
+    tokens.arrive(1, 0)
+    halo_copy(1, 2).start()
     for i in range(ZL - 1):
         wo_z(i).wait_recv()
     for i in range(X - 1):
         wo_x(i).start()
-    for c in range(1, PIECES):
-        tokens.arrive(0, c)
-    tokens.forward(1, 0)
-    halo_copy(1, 1).start()
-    halo_copy(1, 3).start()
-    tokens.spread(1, 2)
-    project(0, 2)
-    tokens.forward(1, 1)
-    tokens.arrive(1, 0)
-    halo_copy(1, 2).start()
     tokens.spread(1, 3)
     project(1, 0)
-    for i in range(X - 1):
-        wo_x(i).wait_recv()
-    wo_core().start()
     tokens.forward(1, 2)
     tokens.forward(1, 3)
     project(1, 1)
@@ -264,19 +295,23 @@
 
     for h in range(HV):
         lanes = pl.ds(LANES * h, LANES)
-
-        @pl.loop(0, T)
-        def _(t):
-            streams = []
+        taps = [[w_short[j, pl.ds(g, 1), lanes] for j in range(3)] for g in range(3)]
+
+        def plane(g, t):
+            return pb[g, h, pl.ds(HALO + t, NCH, stride=T), :]
+
+        def filtered(t, kept):
+            streams, keep = [], []
             for g in range(3):
-                total = None
-                for j in range(3):
-                    plane = pb[g, h, pl.ds(HALO + t - j, NCH, stride=T), :]
-                    term = w_short[j, pl.ds(g, 1), lanes] * plane
-                    total = term if total is None else total + term
-                streams.append(total)
+                now = plane(g, t)
+                older, old = kept[2 * g:2 * g + 2]
+                streams.append(taps[g][0] * now + taps[g][1] * old + taps[g][2] * older)
+                keep += [old, now]
             qb[h, t] = streams[0]
             xb[h, t] = streams[1] * streams[2]
+            return tuple(keep)
+
+        lax.fori_loop(0, T, filtered, tuple(plane(g, t) for g in range(3) for t in (-2, -1)), unroll=2)
 
     group = 4
     for h in range(HV):
@@ -287,7 +322,7 @@
                 value = xb[h, t]
                 return tuple(f * s + value for f, s in zip(factors, states))
 
-            states = lax.fori_loop(0, T, step, tuple(jnp.zeros((NCH, LANES), F32) for _ in factors))
+            states = lax.fori_loop(0, T, step, tuple(jnp.zeros((NCH, LANES), F32) for _ in factors), unroll=4)
             for i, s in enumerate(states):
                 eb[h, (r0 + i) * NCH:(r0 + i + 1) * NCH, :] = s
 
@@ -299,7 +334,7 @@
             sb[h, pl.ds(pl.multiple_of(n * MODES, MODES), MODES), :] = state
             return chunk_decay * state + eb[h, pl.ds(n, MODES, stride=NCH), :]
 
-        block_end.append(lax.fori_loop(0, NCH, scan, jnp.zeros((MODES, LANES), F32)))
+        block_end.append(lax.fori_loop(0, NCH, scan, jnp.zeros((MODES, LANES), F32), unroll=4))
     mine = jnp.concatenate(block_end, axis=1)
 
     st_core[0] = mine
@@ -324,6 +359,14 @@
                 term = ft[h, lag:lag + 1, :] * xb[h, t - lag]
                 total = term if total is None else total + term
             yb[h, t] = total
+
+    for h in range(HV):
+        front = res[:, LANES * h:LANES * (h + 1)] * ab[h]
+
+        @pl.loop(0, NCH)
+        def _(n):
+            at = pl.ds(pl.multiple_of(n * MODES, MODES), MODES)
+            sb[h, at, :] = front * sb[h, at, :]
 
     within(0)
     for copy in z_copies:
@@ -350,6 +393,9 @@
     before_chip = jnp.exp(-dec[...] * (ROWS * CORES * zl).astype(F32))
     for copy in x_copies:
         copy.wait_recv()
+    for i in range(X - 1):
+        wo_x(i).wait_recv()
+    wo_core().start()
     line_in = jnp.zeros((MODES, CHL), F32)
     for xx in range(X):
         for a in range(X):
@@ -363,33 +409,30 @@
     chip_in = chip_in + before_chip * line_in
     carried = jnp.where(core == 0, chip_in, decay_block * chip_in + theirs)
 
-    for h in range(HV):
-        part = slice(LANES * h, LANES * (h + 1))
-        chunk_decay = jnp.exp(-dec[:, part] * float(T))
-        front = res[:, part] * ab[h]
-
-        def enter(n, state):
-            at = pl.ds(pl.multiple_of(n * MODES, MODES), MODES)
-            sb[h, at, :] = front * (sb[h, at, :] + state)
-            return chunk_decay * state
-
-        lax.fori_loop(0, NCH, enter, carried[:, part])
-        for r0 in range(0, MODES, group):
-            factors = [jnp.broadcast_to(ab[h, r:r + 1, :], (NCH, LANES)) for r in range(r0, r0 + group)]
-            start = tuple(sb[h, pl.ds(r, NCH, stride=MODES), :] for r in range(r0, r0 + group))
-            last = r0 + group == MODES
+    st_in[...] = carried
+    per = NCH // PIECES
+
+    def gate(c):
+        n0 = per * (PIECES - 1 - c)
+        for h in range(HV):
+            lanes = pl.ds(LANES * h, LANES)
+            factors, start = [], []
+            for r in range(MODES):
+                at = pl.ds(n0 * MODES + r, per, stride=MODES)
+                factors.append(jnp.broadcast_to(ab[h, r:r + 1, :], (per, LANES)))
+                start.append(sb[h, at, :] + pw[h, at, :] * st_in[r:r + 1, lanes])
 
             def step(t, terms):
-                total = yb[h, t] + sum(terms[1:], terms[0])
-                if last:
-                    gb[h, pl.ds(t, NCH, stride=T), :] = qb[h, t] * total
-                else:
-                    yb[h, t] = total
+                sums = list(terms)
+                while len(sums) > 1:
+                    sums = [a + b for a, b in zip(sums[::2], sums[1::2])]
+                total = yb[h, t, pl.ds(n0, per), :] + sums[0]
+                gb[h, pl.ds(n0 * T + t, per, stride=T), :] = qb[h, t, pl.ds(n0, per), :] * total
                 return tuple(f * s for f, s in zip(factors, terms))
 
-            lax.fori_loop(0, T, step, start)
-    for h in range(HV):
-        own[:, LANES * h:LANES * (h + 1)] = gb[h].astype(BF16)
+            lax.fori_loop(0, T, step, tuple(start), unroll=2)
+        for h in range(HV):
+            own[rows_of(c), LANES * h:LANES * (h + 1)] = gb[h, rows_of(c), :].astype(BF16)
 
     gates = Gather(own, gg, s2, r2)
 
@@ -403,26 +446,38 @@
         else:
             oacc[...] += value
 
-    gates.cross()
-    for c in range(PIECES):
-        gates.spread(0, c)
+    gate(0)
+    gates.cross(0)
+    gates.spread(0, 0)
+    gate(1)
+    gates.spread(0, 1)
+    gate(2)
+    gate(3)
+    gates.spread(0, 2)
+    gates.cross(1)
+    gates.forward(0, 0)
     wo_core().wait_recv()
     emit(0, 0, first=True)
-    for c in range(PIECES):
-        gates.forward(0, c)
-        if c >= 2:
-            gates.spread(1, c - 2)
+    gates.spread(0, 3)
+    gates.forward(0, 1)
+    gates.cross(2)
+    gates.forward(0, 2)
+    gates.spread(1, 0)
+    gates.forward(0, 3)
+    gates.cross(3)
     emit(0, 1)
     emit(0, 3)
+    gates.spread(1, 1)
+    gates.forward(1, 0)
     for c in range(PIECES):
         gates.arrive(0, c)
     gates.spread(1, 2)
     emit(0, 2)
-    gates.forward(1, 0)
+    gates.forward(1, 1)
     gates.spread(1, 3)
     emit(1, 0)
-    for c in range(1, PIECES):
-        gates.forward(1, c)
+    gates.forward(1, 2)
+    gates.forward(1, 3)
     emit(1, 1)
     emit(1, 3)
     for c in range(PIECES):
@@ -434,8 +489,11 @@
     for p in range(ZH):
         for s in range(Y):
             halo_copy(p, s).wait_send()
-    for i in range(N_TP - 1):
-        wo_first(i).wait_send()
+    for b in range(Y):
+        wo_across(b).wait_send()
+    for b in range(1, Y):
+        wo_y(b).wait_send()
+        wo_relayed(b).wait_send()
     for i in range(ZL - 1):
         wo_z(i).wait_send()
     for i in range(X - 1):
@@ -452,7 +510,7 @@
     hbm = pl.BlockSpec(memory_space=pl.ANY)
     return pl.pallas_call(
         kernel,
-        out_shape=jax.ShapeDtypeStruct((ROWS, FEAT), BF16),
+        out_shape=pltpu.VMEM((ROWS, FEAT), BF16),
         in_specs=[vmem, vmem, hbm, vmem, vmem, vmem, vmem, hbm],
         out_specs=vmem,
         scratch_shapes=[
@@ -470,18 +528,21 @@
             pltpu.VMEM((HV, MODES, LANES), F32),
             pltpu.VMEM((HV, MODES * NCH, LANES), F32),
             pltpu.VMEM((HV, MODES * NCH, LANES), F32),
+            pltpu.VMEM((HV, MODES * NCH, LANES), F32),
             pltpu.VMEM((HV, ROWS, LANES), F32),
             pltpu.VMEM((ROWS, CHL), BF16),
             pltpu.VMEM((ZH, Y, ROWS, CHL), BF16),
             pltpu.VMEM((N_TP, CHL, FEAT), BF16),
+            pltpu.VMEM((Y - 1, HALO, CHL), BF16),
             pltpu.VMEM((ROWS, FEAT), F32),
             pltpu.VMEM((2, MODES, CHL), F32),
             pltpu.VMEM((ZL, MODES, CHL), F32),
             pltpu.VMEM((X, MODES, CHL), F32),
+            pltpu.VMEM((MODES, CHL), F32),
             dma((5, 2, PIECES)), dma((5, 2, PIECES)),
             dma((5, 2, PIECES)), dma((5, 2, PIECES)),
             dma((ZH, Y)), dma((ZH, Y)),
-            dma((N_TP - 1,)), dma((N_TP - 1,)),
+            dma((3 * Y - 2,)), dma((3 * Y - 2,)),
             dma((ZL - 1,)), dma((ZL - 1,)),
             dma((X - 1,)), dma((X - 1,)),
             dma((1,)), dma((1,)),

time: 105 us -> 90.4 us (0.86)
  the two profiles are of different devices: /device:TPU:76 before, /device:TPU:2 now
where the time goes in v2:
time: 90.4 us; the launch traced here: 89.6 us
  Pallas kernels  88.8 us (98%)
    pallas_call x1, Pallas kernels, local(): pl.pallas_call(kernel, out_shape=pltpu.VMEM((ROWS, FEAT), BF16), in_specs...  88.8 us

profile of v2, /device:TPU:2, one launch (start us, length us, event | category | flops | bytes accessed | tf_op | source)
XLA Modules:
  0.0 89.6 jit_solution(3660115289701449900)
XLA Ops:
  0.0 88.8 %hyena.1 = bf16[512,512]{1,0:T(8,128)(2,1)S(1)} custom-call(bf16[512,512]{1,0:T(8,128)(2,1)} %tok.1, f32[32,128]{1,0:T(8,128)} %bitcast.6, bf16[3,4096,256]{2,1,0:T(8,128)(2,1)} %bitcast.5, f32[3,3,256]{2,1,0:T(4,128)} %w_short.1, f32[16,256]{1,0:T(8,128)} %bitcast.7, f32[16,256]{1,0:T(8,128)} %bitcast.8, f32[1,256]{1,0:T(1,128)} %bitcast.9, ...), custom_call_target="tpu_custom_call" | custom-call | tf_op jit(solution)/shard_map/hyena/pallas_call | solution.py:511
  88.8 0.8 copy.10

commit v3 on v2

--- a/solution.py
+++ b/solution.py
@@ -18,11 +18,8 @@
 D = 4096
 CHL = 256
 MODES = 16
-PIECES = 4
-PROWS = ROWS // PIECES
-HALF = PROWS // 2
+GATED = 4
 HALO = 16
-WINDOW = 2
 EXT = ROWS + HALO
 T = 16
 NCH = ROWS // T
@@ -37,7 +34,8 @@
 
 
 def kernel(
-    tok, gain, w_in, w_short, res, dec, direct, w_out, out,
+    tok_in, gain_in, w_in, taps_in, res_in, dec_in, direct_in, w_out, out,
+    gain, w_short, res, dec, direct,
     xg, halo, wv, xs, ssq, acc, pb, qb, xb, yb, ft, ab, eb, sb, pw, gb, own, gg, wo, wt, oacc,
     st_core, st_z, st_x, st_in,
     s1, r1, s2, r2, hs, hr, ws, wr, zs, zr, xsnd, xrcv, cs, cr, es, er, lsem,
@@ -62,53 +60,59 @@
     after = ((ctx + 1) % N_CTX, tp)
     before = ((ctx + N_CTX - 1) % N_CTX, tp)
 
-    w_load = pltpu.make_async_copy(w_in, wv, lsem.at[0])
-    w_load.start()
-
     barrier = pltpu.get_barrier_semaphore()
     greeted = y_dev + z_dev + x_dev + [across, other, after, before]
     for device in greeted:
         pl.semaphore_signal(barrier, inc=1, device_id=device, device_id_type=MESH)
+    small = [(gain_in, gain), (taps_in, w_short), (res_in, res), (dec_in, dec), (direct_in, direct)]
+    tok = xg.at[0, 0]
+    loads = [pltpu.make_async_copy(a, b, lsem.at[2 + i]) for i, (a, b) in enumerate([(tok_in, tok)] + small)]
+    for load in loads:
+        load.start()
+    w_load = pltpu.make_async_copy(w_in, wv, lsem.at[0])
+    w_load.start()
+    for load in loads:
+        load.wait()
     pl.semaphore_wait(barrier, len(greeted))
 
-    def rows_of(c, half=None):
-        start = ROWS - PROWS * (c + 1)
-        if half is None:
-            return pl.ds(start, PROWS)
-        return pl.ds(start + half * HALF, HALF)
-
     class Gather:
-        def __init__(self, mine, buf, send, recv):
+        def __init__(self, mine, buf, send, recv, pieces, window, crossing):
             self.mine, self.buf, self.send, self.recv = mine, buf, send, recv
+            self.pieces, self.window, self.crossing = pieces, window, crossing
             self.queue = []
+
+        def rows(self, c, half=None):
+            size = ROWS // self.pieces
+            start = ROWS - size * (c + 1)
+            return pl.ds(start, size) if half is None else pl.ds(start + half * (size // 2), size // 2)
 
         def held(self, p, s):
             return self.mine if (p, s) == (0, 0) else self.buf.at[p, s]
 
         def copy(self, kind, p, c):
             if kind == 0:
-                src, dst, dev = self.held(p, 0).at[rows_of(c)], self.buf.at[p, 1, rows_of(c)], right
+                src, dst, dev = self.held(p, 0).at[self.rows(c)], self.buf.at[p, 1, self.rows(c)], right
             elif kind == 1:
-                src, dst, dev = self.held(p, 0).at[rows_of(c)], self.buf.at[p, 3, rows_of(c)], left
+                src, dst, dev = self.held(p, 0).at[self.rows(c)], self.buf.at[p, 3, self.rows(c)], left
             elif kind == 2:
-                src, dst, dev = self.buf.at[p, 1, rows_of(c, 0)], self.buf.at[p, 2, rows_of(c, 0)], right
+                src, dst, dev = self.buf.at[p, 1, self.rows(c, 0)], self.buf.at[p, 2, self.rows(c, 0)], right
             elif kind == 3:
-                src, dst, dev = self.buf.at[p, 3, rows_of(c, 1)], self.buf.at[p, 2, rows_of(c, 1)], left
+                src, dst, dev = self.buf.at[p, 3, self.rows(c, 1)], self.buf.at[p, 2, self.rows(c, 1)], left
             else:
-                src, dst, dev = self.mine.at[rows_of(c)], self.buf.at[1, 0, rows_of(c)], across
+                src, dst, dev = self.mine.at[self.rows(c)], self.buf.at[1, 0, self.rows(c)], across
             return remote(src, dst, self.send.at[kind, p, c], self.recv.at[kind, p, c], dev)
 
         def push(self, *copies):
-            if len(self.queue) >= WINDOW:
-                for copy in self.queue[-WINDOW]:
+            if len(self.queue) >= self.window:
+                for copy in self.queue[-self.window]:
                     copy.wait_send()
             for copy in copies:
                 copy.start()
             self.queue.append(copies)
 
         def cross(self, c):
-            if c:
-                self.copy(4, 0, c - 1).wait_send()
+            if c >= self.crossing:
+                self.copy(4, 0, c - self.crossing).wait_send()
             self.copy(4, 0, c).start()
 
         def spread(self, p, c):
@@ -126,15 +130,16 @@
             self.copy(3, p, c).wait_recv()
 
         def sent(self):
-            self.copy(4, 0, PIECES - 1).wait_send()
-            for copies in self.queue[-WINDOW:]:
+            for c in range(self.pieces - self.crossing, self.pieces):
+                self.copy(4, 0, c).wait_send()
+            for copies in self.queue[-self.window:]:
                 for copy in copies:
                     copy.wait_send()
 
     def owner(p, s):
         return (zh + p) % ZH * Y + (y + (0, Y - 1, 2, 1)[s]) % Y
 
-    tokens = Gather(tok, xg, s1, r1)
+    tokens = Gather(tok, xg, s1, r1, 4, 2, 1)
 
     def halo_copy(p, s):
         return remote(
@@ -142,41 +147,54 @@
         )
 
     chip = x * ZL + zl
-    lane0 = pl.multiple_of(core * CHL, CHL)
 
     wo_rows = pl.ds(pl.multiple_of(chip * HALO, HALO), HALO)
-    wo_lanes = pl.ds(lane0, CHL)
 
     def wo_columns(device):
         return w_out.at[wo_rows, pl.ds(pl.multiple_of(device[1] * FEAT + core * CHL, CHL), CHL)]
 
     def wo_across(b):
-        dst = wt.at[b - 1] if b else wo.at[tp, wo_rows, wo_lanes]
+        dst = wt.at[b - 1] if b else wo.at[core, chip, tp]
         return remote(wo_columns(at_tp(1 - zh, (y + b) % Y)), dst, ws.at[b], wr.at[b], across)
 
     def wo_y(b):
-        dst = wo.at[tp, wo_rows, wo_lanes]
+        dst = wo.at[core, chip, tp]
         return remote(wo_columns(y_dev[b - 1]), dst, ws.at[Y + b - 1], wr.at[Y + b - 1], y_dev[b - 1])
 
     def wo_relayed(b):
-        dst = wo.at[across[1], wo_rows, wo_lanes]
+        dst = wo.at[core, chip, across[1]]
         at = 2 * Y + b - 2
         return remote(wt.at[b - 1], dst, ws.at[at], wr.at[at], y_dev[b - 1])
 
     def wo_mine():
-        return pltpu.make_async_copy(wo_columns((ctx, tp)), wo.at[tp, wo_rows, wo_lanes], lsem.at[1])
-
-    def wo_z(i):
-        part = wo.at[:, wo_rows, wo_lanes]
-        return remote(part, part, zs.at[i], zr.at[i], z_dev[i])
-
-    def wo_x(i):
-        part = wo.at[:, pl.ds(pl.multiple_of(x * ZL * HALO, ZL * HALO), ZL * HALO), wo_lanes]
-        return remote(part, part, xsnd.at[i], xrcv.at[i], x_dev[i])
-
-    def wo_core():
-        part = wo.at[:, :, wo_lanes]
-        return remote(part, part, cs.at[0], cr.at[0], other)
+        return pltpu.make_async_copy(wo_columns((ctx, tp)), wo.at[core, chip, tp], lsem.at[1])
+
+    def groups(part):
+        return pl.ds(part * (N_TP // 2), N_TP // 2)
+
+    def wo_z(part):
+        block = wo.at[core, chip, groups(part)]
+        return [remote(block, block, zs.at[part, i], zr.at[part, i], z_dev[i]) for i in range(ZL - 1)]
+
+    def wo_x(part):
+        block = wo.at[core, pl.ds(x * ZL, ZL), groups(part)]
+        return [remote(block, block, xsnd.at[part, i], xrcv.at[part, i], x_dev[i]) for i in range(X - 1)]
+
+    def start(copies):
+        for copy in copies:
+            copy.start()
+
+    def landed(copies):
+        for copy in copies:
+            copy.wait_recv()
+
+    def left_here(copies):
+        for copy in copies:
+            copy.wait_send()
+
+    def wo_core(part):
+        block = wo.at[core, :, groups(part)]
+        return [remote(block, block, cs.at[part], cr.at[part], other)]
 
     def project(p, s):
         halo_copy(p, s).wait_recv()
@@ -204,11 +222,6 @@
     tokens.spread(0, 0)
     tokens.spread(0, 1)
     halo_copy(0, 0).start()
-    for b in range(Y):
-        wo_across(b).start()
-    for b in range(1, Y):
-        wo_y(b).start()
-    wo_mine().start()
 
     ssq[...] = jnp.zeros_like(ssq)
     acc[...] = jnp.zeros_like(acc)
@@ -245,9 +258,6 @@
     halo_copy(0, 2).start()
     tokens.cross(2)
     tokens.forward(0, 2)
-    for b in range(1, Y):
-        wo_across(b).wait_recv()
-        wo_relayed(b).start()
     tokens.forward(0, 3)
     tokens.spread(1, 0)
     halo_copy(1, 0).start()
@@ -255,34 +265,37 @@
     tokens.spread(1, 1)
     tokens.cross(3)
     project(0, 3)
-    for c in range(1, PIECES):
+    for c in range(1, 4):
         tokens.arrive(0, c)
     project(0, 2)
     tokens.forward(1, 0)
     halo_copy(1, 1).start()
     halo_copy(1, 3).start()
     tokens.spread(1, 2)
+    tokens.forward(1, 1)
+    tokens.arrive(1, 0)
+    halo_copy(1, 2).start()
+    for b in range(Y):
+        wo_across(b).start()
+    for b in range(1, Y):
+        wo_y(b).start()
+    wo_mine().start()
+    tokens.spread(1, 3)
+    project(1, 0)
+    tokens.forward(1, 2)
+    for b in range(1, Y):
+        wo_across(b).wait_recv()
+        wo_relayed(b).start()
+    tokens.forward(1, 3)
+    project(1, 1)
+    project(1, 3)
     wo_mine().wait()
     wo_across(0).wait_recv()
     for b in range(1, Y):
         wo_y(b).wait_recv()
         wo_relayed(b).wait_recv()
-    for i in range(ZL - 1):
-        wo_z(i).start()
-    tokens.forward(1, 1)
-    tokens.arrive(1, 0)
-    halo_copy(1, 2).start()
-    for i in range(ZL - 1):
-        wo_z(i).wait_recv()
-    for i in range(X - 1):
-        wo_x(i).start()
-    tokens.spread(1, 3)
-    project(1, 0)
-    tokens.forward(1, 2)
-    tokens.forward(1, 3)
-    project(1, 1)
-    project(1, 3)
-    for c in range(1, PIECES):
+    start(wo_z(0) + wo_z(1))
+    for c in range(1, 4):
         tokens.arrive(1, c)
     project(1, 2)
 
@@ -393,9 +406,8 @@
     before_chip = jnp.exp(-dec[...] * (ROWS * CORES * zl).astype(F32))
     for copy in x_copies:
         copy.wait_recv()
-    for i in range(X - 1):
-        wo_x(i).wait_recv()
-    wo_core().start()
+    landed(wo_z(0) + wo_z(1))
+    start(wo_x(0) + wo_x(1))
     line_in = jnp.zeros((MODES, CHL), F32)
     for xx in range(X):
         for a in range(X):
@@ -410,17 +422,18 @@
     carried = jnp.where(core == 0, chip_in, decay_block * chip_in + theirs)
 
     st_in[...] = carried
-    per = NCH // PIECES
+    per = NCH // GATED
+    span = ROWS // GATED
 
     def gate(c):
-        n0 = per * (PIECES - 1 - c)
+        n0 = per * (GATED - 1 - c)
         for h in range(HV):
             lanes = pl.ds(LANES * h, LANES)
-            factors, start = [], []
+            factors, terms0 = [], []
             for r in range(MODES):
                 at = pl.ds(n0 * MODES + r, per, stride=MODES)
                 factors.append(jnp.broadcast_to(ab[h, r:r + 1, :], (per, LANES)))
-                start.append(sb[h, at, :] + pw[h, at, :] * st_in[r:r + 1, lanes])
+                terms0.append(sb[h, at, :] + pw[h, at, :] * st_in[r:r + 1, lanes])
 
             def step(t, terms):
                 sums = list(terms)
@@ -430,21 +443,26 @@
                 gb[h, pl.ds(n0 * T + t, per, stride=T), :] = qb[h, t, pl.ds(n0, per), :] * total
                 return tuple(f * s for f, s in zip(factors, terms))
 
-            lax.fori_loop(0, T, step, tuple(start), unroll=2)
+            lax.fori_loop(0, T, step, tuple(terms0), unroll=2)
         for h in range(HV):
-            own[rows_of(c), LANES * h:LANES * (h + 1)] = gb[h, rows_of(c), :].astype(BF16)
-
-    gates = Gather(own, gg, s2, r2)
+            at = pl.ds(ROWS - span * (c + 1), span)
+            own[at, LANES * h:LANES * (h + 1)] = gb[h, at, :].astype(BF16)
+
+    gates = Gather(own, gg, s2, r2, 4, 4, 1)
 
     def emit(p, s, first=False, last=False):
-        weights = wo[owner(p, s)]
-        value = jnp.dot(gates.held(p, s)[...], weights, preferred_element_type=F32)
-        if first:
-            oacc[...] = value
-        elif last:
-            out[...] = (oacc[...] + value).astype(BF16)
-        else:
-            oacc[...] += value
+        k = owner(p, s)
+        block = gates.held(p, s)[...]
+        for half in range(CORES):
+            weights = wo[half, :, k].reshape(CHL, CHL)
+            value = jnp.dot(block, weights, preferred_element_type=F32)
+            lanes = slice(CHL * half, CHL * (half + 1))
+            if first:
+                oacc[:, lanes] = value
+            elif last:
+                out[:, lanes] = (oacc[:, lanes] + value).astype(BF16)
+            else:
+                oacc[:, lanes] += value
 
     gate(0)
     gates.cross(0)
@@ -456,8 +474,6 @@
     gates.spread(0, 2)
     gates.cross(1)
     gates.forward(0, 0)
-    wo_core().wait_recv()
-    emit(0, 0, first=True)
     gates.spread(0, 3)
     gates.forward(0, 1)
     gates.cross(2)
@@ -465,22 +481,26 @@
     gates.spread(1, 0)
     gates.forward(0, 3)
     gates.cross(3)
+    gates.spread(1, 1)
+    gates.forward(1, 0)
+    landed(wo_x(0) + wo_x(1))
+    start(wo_core(0) + wo_core(1))
+    for c in range(4):
+        gates.arrive(0, c)
+    gates.spread(1, 2)
+    landed(wo_core(0) + wo_core(1))
+    emit(0, 0, first=True)
+    gates.forward(1, 1)
     emit(0, 1)
     emit(0, 3)
-    gates.spread(1, 1)
-    gates.forward(1, 0)
-    for c in range(PIECES):
-        gates.arrive(0, c)
-    gates.spread(1, 2)
+    gates.spread(1, 3)
     emit(0, 2)
-    gates.forward(1, 1)
-    gates.spread(1, 3)
     emit(1, 0)
     gates.forward(1, 2)
     gates.forward(1, 3)
     emit(1, 1)
     emit(1, 3)
-    for c in range(PIECES):
+    for c in range(4):
         gates.arrive(1, c)
     emit(1, 2, last=True)
 
@@ -494,11 +514,8 @@
     for b in range(1, Y):
         wo_y(b).wait_send()
         wo_relayed(b).wait_send()
-    for i in range(ZL - 1):
-        wo_z(i).wait_send()
-    for i in range(X - 1):
-        wo_x(i).wait_send()
-    wo_core().wait_send()
+    for part in range(2):
+        left_here(wo_z(part) + wo_x(part) + wo_core(part))
     core_copy.wait_send()
     for copy in z_copies + x_copies:
         copy.wait_send()
@@ -511,9 +528,14 @@
     return pl.pallas_call(
         kernel,
         out_shape=pltpu.VMEM((ROWS, FEAT), BF16),
-        in_specs=[vmem, vmem, hbm, vmem, vmem, vmem, vmem, hbm],
+        in_specs=[hbm] * 8,
         out_specs=vmem,
         scratch_shapes=[
+            pltpu.VMEM((D // LANES, LANES), F32),
+            pltpu.VMEM((3, 3, CHL), F32),
+            pltpu.VMEM((MODES, CHL), F32),
+            pltpu.VMEM((MODES, CHL), F32),
+            pltpu.VMEM((1, CHL), F32),
             pltpu.VMEM((ZH, Y, ROWS, FEAT), BF16),
             pltpu.VMEM((ZH, Y, HALO, FEAT), BF16),
             pltpu.VMEM((3, D, CHL), BF16),
@@ -532,22 +554,22 @@
             pltpu.VMEM((HV, ROWS, LANES), F32),
             pltpu.VMEM((ROWS, CHL), BF16),
             pltpu.VMEM((ZH, Y, ROWS, CHL), BF16),
-            pltpu.VMEM((N_TP, CHL, FEAT), BF16),
+            pltpu.VMEM((CORES, X * ZL, N_TP, HALO, CHL), BF16),
             pltpu.VMEM((Y - 1, HALO, CHL), BF16),
             pltpu.VMEM((ROWS, FEAT), F32),
             pltpu.VMEM((2, MODES, CHL), F32),
             pltpu.VMEM((ZL, MODES, CHL), F32),
             pltpu.VMEM((X, MODES, CHL), F32),
             pltpu.VMEM((MODES, CHL), F32),
-            dma((5, 2, PIECES)), dma((5, 2, PIECES)),
-            dma((5, 2, PIECES)), dma((5, 2, PIECES)),
+            dma((5, 2, 4)), dma((5, 2, 4)),
+            dma((5, 2, 4)), dma((5, 2, 4)),
             dma((ZH, Y)), dma((ZH, Y)),
             dma((3 * Y - 2,)), dma((3 * Y - 2,)),
-            dma((ZL - 1,)), dma((ZL - 1,)),
-            dma((X - 1,)), dma((X - 1,)),
-            dma((1,)), dma((1,)),
+            dma((2, ZL - 1)), dma((2, ZL - 1)),
+            dma((2, X - 1)), dma((2, X - 1)),
+            dma((2,)), dma((2,)),
             dma((ZL + X - 1,)), dma((ZL + X - 1,)),
-            dma((2,)),
+            dma((8,)),
         ],
         compiler_params=pltpu.CompilerParams(
             collective_id=0, has_side_effects=True, vmem_limit_bytes=56 * 1024 * 1024

time: 90.4 us -> 85.3 us (0.944)
  Pallas kernels: 88.8 us -> 84.3 us
    pallas_call x1, Pallas kernels: 88.8 us -> 84.3 us  [local(): pl.pallas_call(kernel, out_shape=pltpu.VMEM((ROWS, FEAT), BF16), in_specs...]
where the time goes in v3:
time: 85.3 us; the launch traced here: 85.1 us
  Pallas kernels  84.3 us (99%)
    pallas_call x1, Pallas kernels, local(): pl.pallas_call(kernel, out_shape=pltpu.VMEM((ROWS, FEAT), BF16), in_specs...  84.3 us

profile of v3, /device:TPU:2, one launch (start us, length us, event | category | flops | bytes accessed | tf_op | source)
XLA Modules:
  0.0 85.1 jit_solution(2586151005186038075)
XLA Ops:
  0.0 84.3 %hyena.1 = bf16[512,512]{1,0:T(8,128)(2,1)S(1)} custom-call(bf16[512,512]{1,0:T(8,128)(2,1)} %tok_in.1, f32[32,128]{1,0:T(8,128)} %bitcast.6, bf16[3,4096,256]{2,1,0:T(8,128)(2,1)} %bitcast.5, f32[3,3,256]{2,1,0:T(4,128)} %taps_in.1, f32[16,256]{1,0:T(8,128)} %bitcast.7, f32[16,256]{1,0:T(8,128)} %bitcast.8, f32[1,256]{1,0:T(1,128)} %bitcast.9, ...), custom_call_target="tpu_custom_call" | custom-call | tf_op jit(solution)/shard_map/hyena/pallas_call | solution.py:528
  84.3 0.8 copy.10

commit v4 on v3

--- a/solution.py
+++ b/solution.py
@@ -61,7 +61,7 @@
     before = ((ctx + N_CTX - 1) % N_CTX, tp)
 
     barrier = pltpu.get_barrier_semaphore()
-    greeted = y_dev + z_dev + x_dev + [across, other, after, before]
+    greeted = [across] + z_dev + x_dev + y_dev + [before, after, other]
     for device in greeted:
         pl.semaphore_signal(barrier, inc=1, device_id=device, device_id_type=MESH)
     small = [(gain_in, gain), (taps_in, w_short), (res_in, res), (dec_in, dec), (direct_in, direct)]
@@ -76,10 +76,14 @@
     pl.semaphore_wait(barrier, len(greeted))
 
     class Gather:
-        def __init__(self, mine, buf, send, recv, pieces, window, crossing):
+        def __init__(self, mine, buf, send, recv, pieces, window, crossing, direct=False):
             self.mine, self.buf, self.send, self.recv = mine, buf, send, recv
             self.pieces, self.window, self.crossing = pieces, window, crossing
             self.queue = []
+            self.direct = direct
+
+        def straight(self, p, c):
+            return self.direct and (p, c) == (1, self.pieces - 1)
 
         def rows(self, c, half=None):
             size = ROWS // self.pieces
@@ -98,6 +102,8 @@
                 src, dst, dev = self.buf.at[p, 1, self.rows(c, 0)], self.buf.at[p, 2, self.rows(c, 0)], right
             elif kind == 3:
                 src, dst, dev = self.buf.at[p, 3, self.rows(c, 1)], self.buf.at[p, 2, self.rows(c, 1)], left
+            elif kind == 5:
+                src, dst, dev = self.held(p, 0).at[self.rows(c)], self.buf.at[p, 2, self.rows(c)], y_dev[1]
             else:
                 src, dst, dev = self.mine.at[self.rows(c)], self.buf.at[1, 0, self.rows(c)], across
             return remote(src, dst, self.send.at[kind, p, c], self.recv.at[kind, p, c], dev)
@@ -118,16 +124,18 @@
         def spread(self, p, c):
             if p == 1:
                 self.copy(4, 0, c).wait_recv()
-            self.push(self.copy(0, p, c), self.copy(1, p, c))
+            more = [self.copy(5, p, c)] if self.straight(p, c) else []
+            self.push(self.copy(0, p, c), self.copy(1, p, c), *more)
 
         def forward(self, p, c):
             self.copy(0, p, c).wait_recv()
             self.copy(1, p, c).wait_recv()
-            self.push(self.copy(2, p, c), self.copy(3, p, c))
+            if not self.straight(p, c):
+                self.push(self.copy(2, p, c), self.copy(3, p, c))
 
         def arrive(self, p, c):
-            self.copy(2, p, c).wait_recv()
-            self.copy(3, p, c).wait_recv()
+            for kind in (5,) if self.straight(p, c) else (2, 3):
+                self.copy(kind, p, c).wait_recv()
 
         def sent(self):
             for c in range(self.pieces - self.crossing, self.pieces):
@@ -196,16 +204,17 @@
         block = wo.at[core, :, groups(part)]
         return [remote(block, block, cs.at[part], cr.at[part], other)]
 
-    def project(p, s):
-        halo_copy(p, s).wait_recv()
+    def project(p, s, lo=0, hi=EXT):
         k = owner(p, s)
         block = tokens.held(p, s)
         scale = jnp.concatenate([gain[pl.ds(4 * k + i, 1), :] for i in range(4)], axis=1)
-        head = halo[p, s].astype(F32)
-        xs[0:HALO, :] = (head * scale).astype(BF16)
-        ssq[0:HALO, :] += sum(jnp.square(head[:, LANES * i:LANES * (i + 1)]) for i in range(4))
-
-        @pl.loop(0, ROWS // 64)
+        if lo == 0:
+            halo_copy(p, s).wait_recv()
+            head = halo[p, s].astype(F32)
+            xs[0:HALO, :] = (head * scale).astype(BF16)
+            ssq[0:HALO, :] += sum(jnp.square(head[:, LANES * i:LANES * (i + 1)]) for i in range(4))
+
+        @pl.loop(max(lo - HALO, 0) // 64, (hi - HALO) // 64)
         def _(i):
             at = pl.ds(pl.multiple_of(i * 64, 64), 64)
             to = pl.ds(pl.multiple_of(i * 64 + HALO, HALO), 64)
@@ -216,7 +225,7 @@
         @pl.loop(0, 3)
         def _(g):
             weights = wv[g, pl.ds(pl.multiple_of(k * FEAT, FEAT), FEAT), :]
-            acc[g] += jnp.dot(xs[...], weights, preferred_element_type=F32)
+            acc[g, lo:hi] += jnp.dot(xs[lo:hi], weights, preferred_element_type=F32)
 
     tokens.cross(0)
     tokens.spread(0, 0)
@@ -295,9 +304,11 @@
         wo_y(b).wait_recv()
         wo_relayed(b).wait_recv()
     start(wo_z(0) + wo_z(1))
-    for c in range(1, 4):
-        tokens.arrive(1, c)
-    project(1, 2)
+    tokens.arrive(1, 1)
+    tokens.arrive(1, 2)
+    project(1, 2, HALO + ROWS // 4, EXT)
+    tokens.arrive(1, 3)
+    project(1, 2, 0, HALO + ROWS // 4)
 
     inverse = lax.rsqrt(jnp.sum(ssq[...], axis=1, keepdims=True) * (1.0 / D) + 1e-06)
     row_id = lax.broadcasted_iota(jnp.int32, (EXT, 1), 0)
@@ -406,8 +417,6 @@
     before_chip = jnp.exp(-dec[...] * (ROWS * CORES * zl).astype(F32))
     for copy in x_copies:
         copy.wait_recv()
-    landed(wo_z(0) + wo_z(1))
-    start(wo_x(0) + wo_x(1))
     line_in = jnp.zeros((MODES, CHL), F32)
     for xx in range(X):
         for a in range(X):
@@ -448,7 +457,7 @@
             at = pl.ds(ROWS - span * (c + 1), span)
             own[at, LANES * h:LANES * (h + 1)] = gb[h, at, :].astype(BF16)
 
-    gates = Gather(own, gg, s2, r2, 4, 4, 1)
+    gates = Gather(own, gg, s2, r2, 4, 4, 1, direct=True)
 
     def emit(p, s, first=False, last=False):
         k = owner(p, s)
@@ -467,6 +476,8 @@
     gate(0)
     gates.cross(0)
     gates.spread(0, 0)
+    landed(wo_z(0) + wo_z(1))
+    start(wo_x(0) + wo_x(1))
     gate(1)
     gates.spread(0, 1)
     gate(2)
@@ -562,7 +573,7 @@
             pltpu.VMEM((X, MODES, CHL), F32),
             pltpu.VMEM((MODES, CHL), F32),
             dma((5, 2, 4)), dma((5, 2, 4)),
-            dma((5, 2, 4)), dma((5, 2, 4)),
+            dma((6, 2, 4)), dma((6, 2, 4)),
             dma((ZH, Y)), dma((ZH, Y)),
             dma((3 * Y - 2,)), dma((3 * Y - 2,)),
             dma((2, ZL - 1)), dma((2, ZL - 1)),

time: 85.3 us -> 83.9 us (0.984)
  Pallas kernels: 84.3 us -> 83 us
    pallas_call x1, Pallas kernels: 84.3 us -> 83 us  [local(): pl.pallas_call(kernel, out_shape=pltpu.VMEM((ROWS, FEAT), BF16), in_specs...]
where the time goes in v4:
time: 83.9 us; the launch traced here: 83.8 us
  Pallas kernels  83 us (99%)
    pallas_call x1, Pallas kernels, local(): pl.pallas_call(kernel, out_shape=pltpu.VMEM((ROWS, FEAT), BF16), in_specs...  83 us

profile of v4, /device:TPU:2, one launch (start us, length us, event | category | flops | bytes accessed | tf_op | source)
XLA Modules:
  0.0 83.8 jit_solution(4036684694101342263)
XLA Ops:
  0.0 83.0 %hyena.1 = bf16[512,512]{1,0:T(8,128)(2,1)S(1)} custom-call(bf16[512,512]{1,0:T(8,128)(2,1)} %tok_in.1, f32[32,128]{1,0:T(8,128)} %bitcast.6, bf16[3,4096,256]{2,1,0:T(8,128)(2,1)} %bitcast.5, f32[3,3,256]{2,1,0:T(4,128)} %taps_in.1, f32[16,256]{1,0:T(8,128)} %bitcast.7, f32[16,256]{1,0:T(8,128)} %bitcast.8, f32[1,256]{1,0:T(1,128)} %bitcast.9, ...), custom_call_target="tpu_custom_call" | custom-call | tf_op jit(solution)/shard_map/hyena/pallas_call | solution.py:539
  83.0 0.8 copy.10

commit v5 on v4

--- a/solution.py
+++ b/solution.py
@@ -335,7 +335,7 @@
             xb[h, t] = streams[1] * streams[2]
             return tuple(keep)
 
-        lax.fori_loop(0, T, filtered, tuple(plane(g, t) for g in range(3) for t in (-2, -1)), unroll=2)
+        lax.fori_loop(0, T, filtered, tuple(plane(g, t) for g in range(3) for t in (-2, -1)), unroll=8)
 
     group = 4
     for h in range(HV):
@@ -346,7 +346,7 @@
                 value = xb[h, t]
                 return tuple(f * s + value for f, s in zip(factors, states))
 
-            states = lax.fori_loop(0, T, step, tuple(jnp.zeros((NCH, LANES), F32) for _ in factors), unroll=4)
+            states = lax.fori_loop(0, T, step, tuple(jnp.zeros((NCH, LANES), F32) for _ in factors), unroll=8)
             for i, s in enumerate(states):
                 eb[h, (r0 + i) * NCH:(r0 + i + 1) * NCH, :] = s
 
@@ -358,7 +358,7 @@
             sb[h, pl.ds(pl.multiple_of(n * MODES, MODES), MODES), :] = state
             return chunk_decay * state + eb[h, pl.ds(n, MODES, stride=NCH), :]
 
-        block_end.append(lax.fori_loop(0, NCH, scan, jnp.zeros((MODES, LANES), F32), unroll=4))
+        block_end.append(lax.fori_loop(0, NCH, scan, jnp.zeros((MODES, LANES), F32), unroll=8))
     mine = jnp.concatenate(block_end, axis=1)
 
     st_core[0] = mine
@@ -452,7 +452,7 @@
                 gb[h, pl.ds(n0 * T + t, per, stride=T), :] = qb[h, t, pl.ds(n0, per), :] * total
                 return tuple(f * s for f, s in zip(factors, terms))
 
-            lax.fori_loop(0, T, step, tuple(terms0), unroll=2)
+            lax.fori_loop(0, T, step, tuple(terms0), unroll=8)
         for h in range(HV):
             at = pl.ds(ROWS - span * (c + 1), span)
             own[at, LANES * h:LANES * (h + 1)] = gb[h, at, :].astype(BF16)

time: 83.9 us -> 83.6 us (level)
  no operation moved by 1% of the time
where the time goes in v5:
time: 83.6 us; the launch traced here: 83.5 us
  Pallas kernels  82.7 us (99%)
    pallas_call x1, Pallas kernels, local(): pl.pallas_call(kernel, out_shape=pltpu.VMEM((ROWS, FEAT), BF16), in_specs...  82.7 us

profile of v5, /device:TPU:2, one launch (start us, length us, event | category | flops | bytes accessed | tf_op | source)
XLA Modules:
  0.0 83.5 jit_solution(11252803228060284571)
XLA Ops:
  0.0 82.7 %hyena.1 = bf16[512,512]{1,0:T(8,128)(2,1)S(1)} custom-call(bf16[512,512]{1,0:T(8,128)(2,1)} %tok_in.1, f32[32,128]{1,0:T(8,128)} %bitcast.6, bf16[3,4096,256]{2,1,0:T(8,128)(2,1)} %bitcast.5, f32[3,3,256]{2,1,0:T(4,128)} %taps_in.1, f32[16,256]{1,0:T(8,128)} %bitcast.7, f32[16,256]{1,0:T(8,128)} %bitcast.8, f32[1,256]{1,0:T(1,128)} %bitcast.9, ...), custom_call_target="tpu_custom_call" | custom-call | tf_op jit(solution)/shard_map/hyena/pallas_call | solution.py:539
  82.7 0.8 copy.10
